TPU v7x, 128 devices: a whole 4x4x4 slice. The times are simulated.
128 devices in a mesh: section: 4 (over z), chan: 32 (over x, y, core).
Axes of the slice: x: 4, y: 4, z: 4, core: 2. Of those that a mesh axis runs over, the one named last changes fastest.
Arguments:
- inputs: bfloat16 [4, 256, 4096], P(None, None, 'chan'), may hold values from -6 to 6
- labels: int32 [4, 256], replicated, may hold values from 0 to 2
- conv_weight: bfloat16 [4, 9, 64, 4096], P('section', None, None, 'chan'), may hold values from -0.25 to 0.25
- point_weight: bfloat16 [4, 4096, 4096], P('section', 'chan'), may hold values from -0.1875 to 0.1875
- head_weight: bfloat16 [4096, 3], P('chan'), may hold values from -0.09375 to 0.09375
Outputs:
- grad_point: float32 [4, 4096, 4096], P('section', 'chan')
- grad_conv: float32 [4, 9, 64, 4096], P('section', None, None, 'chan')
All inputs are finite; a program needn't handle non-finite values.
Results may differ from a plain program's by a relative error of at most 0.035.
Values may be sent and summed in bfloat16 or wider, within the bound.
A program may use at most 128 MiB of HBM per device.

v0:
```python
import jax
import jax.numpy as jnp
from jax import lax
from jax.sharding import PartitionSpec as P

CLASSES = 3
LOSS_SCALE = 2048


def from_behind(value, axis, steps):
    count = lax.axis_size(axis)
    leading, last = (max(0, -steps), min(count, count - steps))
    return lax.ppermute(value, axis, [(source, source + steps) for source in range(leading, last)])


def conv_local(field, kernel, groups):
    half = kernel.shape[0] // 2
    return lax.conv_general_dilated(
        field[None],
        kernel,
        (1,),
        [(half, half)],
        dimension_numbers=("NWC", "WIO", "NWC"),
        feature_group_count=groups,
        preferred_element_type=jnp.float32,
    )[0]


def turn_kernel(kernel):
    taps, width, chans = kernel.shape
    shaped = kernel.reshape(taps, width, chans // width, width)
    shaped = jnp.transpose(shaped, (0, 3, 2, 1))[::-1]
    return shaped.reshape(taps, width, chans)


def kernel_grad(field, grads, width, taps):
    half = taps // 2
    steps, chans = field.shape
    padded = jnp.pad(field, ((half, half), (0, 0)))
    grads3 = grads.reshape(steps, chans // width, width)
    pieces = []
    for k in range(taps):
        shifted = padded[k : k + steps].reshape(steps, chans // width, width)
        pieces.append(
            jnp.einsum("tgi,tgo->igo", shifted, grads3, preferred_element_type=jnp.float32).reshape(
                width, chans
            )
        )
    return jnp.stack(pieces)


def local(inputs, labels, conv_weight, point_weight, head_weight):
    micro, steps, local_chans = inputs.shape
    blocks_here, taps, width, unused_chans = conv_weight.shape
    groups = local_chans // width
    section = lax.axis_index("section")
    n_section = lax.axis_size("section")
    last = n_section - 1
    rounds = micro + n_section - 1
    head32 = head_weight.astype(jnp.float32)
    kernels = [conv_weight[0]]
    turned = [turn_kernel(kernels[0])]
    saved = jnp.zeros((blocks_here, micro, steps, local_chans), jnp.bfloat16)
    top_saved = jnp.zeros((micro, steps, local_chans), jnp.bfloat16)
    received = jnp.zeros((steps, local_chans), jnp.bfloat16)
    for step in range(rounds):
        index = step - section
        valid = (index >= 0) & (index < micro)
        clipped = jnp.clip(index, 0, micro - 1)
        state = jnp.where(
            section == 0, lax.dynamic_index_in_dim(inputs, clipped, 0, keepdims=False), received
        )
        b = 0
        slot = jnp.where(
            valid, lax.dynamic_update_index_in_dim(saved[b], state, clipped, 0), saved[b]
        )
        saved = saved.at[b].set(slot)
        conv_out = conv_local(state, kernels[b], groups)
        act = (conv_out * jax.nn.sigmoid(conv_out)).astype(jnp.bfloat16)
        weight_now = point_weight[b]
        partial_mix = jnp.dot(act, weight_now, preferred_element_type=jnp.float32)
        mixed = lax.psum_scatter(
            partial_mix.astype(jnp.bfloat16), "chan", scatter_dimension=1, tiled=True
        ).astype(jnp.float32)
        state = (state.astype(jnp.float32) + mixed).astype(jnp.bfloat16)
        scores = lax.psum(jnp.dot(state, head_weight, preferred_element_type=jnp.float32), "chan")
        label_row = lax.dynamic_index_in_dim(labels, clipped, 0, keepdims=False)
        onehot = (label_row[:, None] == jnp.arange(CLASSES)[None, :]).astype(jnp.float32)
        top = (jax.nn.sigmoid(scores) - onehot) * (LOSS_SCALE / (micro * steps))
        back_top = jnp.dot(top, head32.T, precision=lax.Precision.HIGHEST).astype(jnp.bfloat16)
        top_saved = jnp.where(
            valid & (section == last),
            lax.dynamic_update_index_in_dim(top_saved, back_top, clipped, 0),
            top_saved,
        )
        if step + 1 < rounds:
            received = from_behind(state, "section", 1)
    grad_point = [jnp.zeros(point_weight.shape[1:], jnp.float32)]
    grad_conv = [jnp.zeros(conv_weight.shape[1:], jnp.float32)]
    received = jnp.zeros((steps, local_chans), jnp.bfloat16)
    for step in range(rounds):
        index = step - (last - section)
        valid = (index >= 0) & (index < micro)
        clipped = jnp.clip(index, 0, micro - 1)
        back = jnp.where(
            section == last,
            lax.dynamic_index_in_dim(top_saved, clipped, 0, keepdims=False),
            received,
        )
        b = 0
        state_b = lax.dynamic_index_in_dim(saved[b], clipped, 0, keepdims=False)
        conv_out = conv_local(state_b, kernels[b], groups)
        sig = jax.nn.sigmoid(conv_out)
        act = jnp.where(valid, (conv_out * sig).astype(jnp.bfloat16), jnp.zeros_like(state_b))
        weight_rows = point_weight[b]

        def fold_grad(carry, piece, start, act=act, weight_rows=weight_rows):
            act_grad, grad_rows_acc = carry
            count = piece.shape[1]
            columns = lax.dynamic_slice_in_dim(weight_rows, start, count, 1)
            act_grad = act_grad + lax.dot_general(
                piece, columns, (((1,), (1,)), ((), ())), preferred_element_type=jnp.float32
            )
            old = lax.dynamic_slice_in_dim(grad_rows_acc, start, count, 1)
            fresh = old + lax.dot_general(
                act, piece, (((0,), (0,)), ((), ())), preferred_element_type=jnp.float32
            )
            return (act_grad, lax.dynamic_update_slice_in_dim(grad_rows_acc, fresh, start, 1))

        start_grad = jnp.zeros((steps, local_chans), jnp.float32)
        act_grad, grad_point[b] = fold_grad(
            (start_grad, grad_point[b]),
            lax.all_gather(back, "chan", axis=1, tiled=True),
            jnp.int32(0),
        )
        conv_grad = jnp.where(
            valid,
            (act_grad * sig * (1.0 + conv_out * (1.0 - sig))).astype(jnp.bfloat16),
            jnp.zeros_like(state_b),
        )
        grad_conv[b] = grad_conv[b] + kernel_grad(state_b, conv_grad, width, taps)
        input_grad = conv_local(conv_grad, turned[b], groups)
        back = (back.astype(jnp.float32) + input_grad).astype(jnp.bfloat16)
        if step + 1 < rounds:
            received = from_behind(back, "section", -1)
    return (jnp.stack(grad_point), jnp.stack(grad_conv))


def solution(mesh):
    placed = (
        P(None, None, "chan"),
        P(),
        P("section", None, None, "chan"),
        P("section", "chan", None),
        P("chan", None),
    )
    return jax.shard_map(
        local,
        mesh=mesh,
        in_specs=placed,
        out_specs=(P("section", "chan", None), P("section", None, None, "chan")),
        check_vma=False,
    )
```

profile of v0, /device:TPU:1, one launch (start us, length us, event | category | flops | bytes accessed | tf_op | source)
XLA Modules:
  0.0 1214.2 jit_solution(8191468728960456842)
XLA Ops:
  12.1 2.5 copy.952
  14.8 80.2 %reduce-scatter.22.cloned.1.call-done = bf16[128,256]{1,0:T(8,128)(2,1)} async-done(((bf16[4096,256]{1,0:T(8,128)(2,1)}), bf16[128,256]{1,0:T(8,128)(2,1)}) %reduce-scatter.22.cloned.1.call-update) | async-done | bytes 65552
  96.0 3.2 collective-permute-start
  104.7 2.5 copy.954
  108.1 79.0 %reduce-scatter.24.cloned.1.call-done = bf16[128,256]{1,0:T(8,128)(2,1)} async-done(((bf16[4096,256]{1,0:T(8,128)(2,1)}), bf16[128,256]{1,0:T(8,128)(2,1)}) %reduce-scatter.24.cloned.1.call-update) | async-done | bytes 65552
  188.1 3.2 collective-permute-start.1
  196.9 2.5 copy.956
  200.3 79.0 %reduce-scatter.26.cloned.1.call-done = bf16[128,256]{1,0:T(8,128)(2,1)} async-done(((bf16[4096,256]{1,0:T(8,128)(2,1)}), bf16[128,256]{1,0:T(8,128)(2,1)}) %reduce-scatter.26.cloned.1.call-update) | async-done | bytes 65552
  280.3 3.3 collective-permute-start.2
  289.0 2.5 copy.958
  292.4 79.0 %reduce-scatter.28.cloned.1.call-done = bf16[128,256]{1,0:T(8,128)(2,1)} async-done(((bf16[4096,256]{1,0:T(8,128)(2,1)}), bf16[128,256]{1,0:T(8,128)(2,1)}) %reduce-scatter.28.cloned.1.call-update) | async-done | bytes 65552
  372.4 3.2 collective-permute-start.3
  381.2 2.5 copy.960
  384.6 79.0 %reduce-scatter.30.cloned.1.call-done = bf16[128,256]{1,0:T(8,128)(2,1)} async-done(((bf16[4096,256]{1,0:T(8,128)(2,1)}), bf16[128,256]{1,0:T(8,128)(2,1)}) %reduce-scatter.30.cloned.1.call-update) | async-done | bytes 65552
  464.6 3.2 collective-permute-start.4
  473.3 2.5 copy.962
  476.7 78.9 %reduce-scatter.32.cloned.1.call-done = bf16[128,256]{1,0:T(8,128)(2,1)} async-done(((bf16[4096,256]{1,0:T(8,128)(2,1)}), bf16[128,256]{1,0:T(8,128)(2,1)}) %reduce-scatter.32.cloned.1.call-update) | async-done | bytes 65552
  556.7 3.4 collective-permute-start.5
  565.4 2.5 copy.964
  569.5 78.3 %reduce-scatter.34.cloned.1.call-done = bf16[128,256]{1,0:T(8,128)(2,1)} async-done(((bf16[4096,256]{1,0:T(8,128)(2,1)}), bf16[128,256]{1,0:T(8,128)(2,1)}) %reduce-scatter.34.cloned.1.call-update) | async-done | bytes 65552
  648.9 121.0 %all-reduce.7 = (f32[256,3]{0,1:T(4,128)S(1)}, f32[256,3]{0,1:T(4,128)S(1)}, f32[256,3]{0,1:T(4,128)S(1)}, f32[256,3]{0,1:T(4,128)S(1)}, f32[256,3]{0,1:T(4,128)...) all-reduce(f32[256,3]{0,1:T(4,128)S(1)} %fusion.205, ...), channel_id=1, replica_groups=mesh['section'=4,'chan'=32] {'chan'}, use_global_device_ids=true, to_apply=%region_6.7 | all-reduce | flops 5376 | bytes 43008 | tf_op jit(solution)/shard_map/psum | solution.py:86
  775.2 44.2 %all-gather.21.cloned.1.call-done = bf16[1,256,4096]{2,1,0:T(8,128)(2,1)} async-done(((bf16[1,256,128]{2,1,0:T(8,128)(2,1)}), bf16[1,256,4096]{2,1,0:T(8,128)(2,1)}) %all-gather.21.cloned.1.call-update) | async-done | bytes 2097168 | tf_op jit(solution)/shard_map/all_gather | solution.py:133
  819.5 2.3 fusion.39
  825.6 3.7 collective-permute-done.6
  832.9 2.2 fusion.195
  836.7 38.7 %all-gather.9.cloned.1.call-done = bf16[256,4096]{1,0:T(8,128)(2,1)} async-done(((bf16[256,128]{1,0:T(8,128)(2,1)}), bf16[256,4096]{1,0:T(8,128)(2,1)}) %all-gather.9.cloned.1.call-update) | async-done | bytes 2097168 | tf_op jit(solution)/shard_map/all_gather | solution.py:133
  875.3 2.3 fusion.47
  881.4 2.3 fusion.199
  940.0 2.3 fusion.46
  946.7 3.1 collective-permute-done.8
  983.5 3.5 convolution_add_fusion.1
  987.2 9.8 all-gather.13.cloned.1.call-done
  997.0 2.3 fusion.45
  1003.5 3.5 collective-permute-done.9
  1010.8 42.2 %all-gather.15.cloned.1.call-done = bf16[256,4096]{1,0:T(8,128)(2,1)} async-done(((bf16[256,128]{1,0:T(8,128)(2,1)}), bf16[256,4096]{1,0:T(8,128)(2,1)}) %all-gather.15.cloned.1.call-update) | async-done | bytes 2097168 | tf_op jit(solution)/shard_map/all_gather | solution.py:133
  1053.1 2.3 fusion.44
  1059.4 3.6 collective-permute-done.10
  1098.7 10.2 all-gather.17.cloned.1.call-done
  1108.9 2.3 fusion.43
  1112.2 3.7 fusion.204
  1122.9 2.3 collective-permute-done.11
  1130.0 3.6 fusion.87
  1161.0 3.5 fusion.85
  1164.6 6.8 all-gather.19.cloned.1.call-done
  1171.3 2.9 fusion.42
  1197.9 2.4 add_add_fusion
  1200.3 2.2 fusion.83
  1203.1 4.0 fusion.4
  (644 shorter events, 273.3 us)
Async XLA Ops:
  7.2 87.8 %reduce-scatter.22.cloned.1.call-start = ((), (), s32[]{:S(2)}) async-start(), calls=%async_computation.14 | async-start | bytes 2162688
  14.5 87.7 %copy-start.32 = (bf16[9,64,2,64]{3,1,2,0:T(8,128)(2,1)S(1)}, bf16[9,64,2,64]{3,1,2,0:T(8,128)(2,1)}, u32[]{:S(2)}) copy-start(bf16[9,64,2,64]{3,1,2,0:T(8,128)(2,1)} %copy-done.31) | copy-start | bytes 442372
  14.6 172.6 %reduce-scatter.24.cloned.1.call-start = ((), (), s32[]{:S(2)}) async-start(), calls=%async_computation.15 | async-start | bytes 2162688
  96.0 4.5 collective-permute-start
  107.2 87.2 %copy-start.33 = (bf16[9,64,2,64]{3,1,2,0:T(8,128)(2,1)S(1)}, bf16[9,64,2,64]{3,1,2,0:T(8,128)(2,1)}, u32[]{:S(2)}) copy-start(bf16[9,64,2,64]{3,1,2,0:T(8,128)(2,1)} %copy-done.31) | copy-start | bytes 442372
  107.2 172.1 %reduce-scatter.26.cloned.1.call-start = ((), (), s32[]{:S(2)}) async-start(), calls=%async_computation.16 | async-start | bytes 2162688
  188.1 4.5 collective-permute-start.1
  199.3 87.2 %copy-start.34 = (bf16[9,64,2,64]{3,1,2,0:T(8,128)(2,1)S(1)}, bf16[9,64,2,64]{3,1,2,0:T(8,128)(2,1)}, u32[]{:S(2)}) copy-start(bf16[9,64,2,64]{3,1,2,0:T(8,128)(2,1)} %copy-done.31) | copy-start | bytes 442372
  199.3 172.1 %reduce-scatter.28.cloned.1.call-start = ((), (), s32[]{:S(2)}) async-start(), calls=%async_computation.17 | async-start | bytes 2162688
  280.3 4.5 collective-permute-start.2
  291.4 87.3 %copy-start.35 = (bf16[9,64,2,64]{3,1,2,0:T(8,128)(2,1)S(1)}, bf16[9,64,2,64]{3,1,2,0:T(8,128)(2,1)}, u32[]{:S(2)}) copy-start(bf16[9,64,2,64]{3,1,2,0:T(8,128)(2,1)} %copy-done.31) | copy-start | bytes 442372
  291.5 172.1 %reduce-scatter.30.cloned.1.call-start = ((), (), s32[]{:S(2)}) async-start(), calls=%async_computation.18 | async-start | bytes 2162688
  372.4 4.5 collective-permute-start.3
  383.6 87.2 %copy-start.36 = (bf16[9,64,2,64]{3,1,2,0:T(8,128)(2,1)S(1)}, bf16[9,64,2,64]{3,1,2,0:T(8,128)(2,1)}, u32[]{:S(2)}) copy-start(bf16[9,64,2,64]{3,1,2,0:T(8,128)(2,1)} %copy-done.31) | copy-start | bytes 442372
  383.7 172.0 %reduce-scatter.32.cloned.1.call-start = ((), (), s32[]{:S(2)}) async-start(), calls=%async_computation.19 | async-start | bytes 2162688
  464.6 4.5 collective-permute-start.4
  475.8 87.2 %copy-start.37 = (bf16[9,64,2,64]{3,1,2,0:T(8,128)(2,1)S(1)}, bf16[9,64,2,64]{3,1,2,0:T(8,128)(2,1)}, u32[]{:S(2)}) copy-start(bf16[9,64,2,64]{3,1,2,0:T(8,128)(2,1)} %copy-done.31) | copy-start | bytes 442372
  475.8 172.0 %reduce-scatter.34.cloned.1.call-start = ((), (), s32[]{:S(2)}) async-start(), calls=%async_computation.20 | async-start | bytes 2162688
  556.7 4.5 collective-permute-start.5
  567.9 205.1 %copy-start.70 = (bf16[1,1,256,128]{3,2,1,0:T(8,128)(2,1)S(1)}, bf16[1,1,256,128]{3,2,1,0:T(8,128)(2,1)}, u32[]{:S(2)}) copy-start(bf16[1,1,256,128]{3,2,1,0:T(8,128)(2,1)} %get-tuple-element.93) | copy-start | bytes 196612
  567.9 205.5 %copy-start.38 = (bf16[9,64,2,64]{3,1,2,0:T(8,128)(2,1)S(1)}, bf16[9,64,2,64]{3,1,2,0:T(8,128)(2,1)}, u32[]{:S(2)}) copy-start(bf16[9,64,2,64]{3,1,2,0:T(8,128)(2,1)} %copy-done.31) | copy-start | bytes 442372
  568.0 251.5 %all-gather.21.cloned.1.call-start = ((), (), s32[]{:S(2)}) async-start(), calls=%async_computation.13 | async-start | bytes 2162688 | tf_op jit(solution)/shard_map/all_gather | solution.py:133
  772.2 177.6 %copy-start.4 = (bf16[4,256,128]{2,1,0:T(8,128)(2,1)}, bf16[4,256,128]{2,1,0:T(8,128)(2,1)S(1)}, u32[]{:S(2)}) copy-start(bf16[4,256,128]{2,1,0:T(8,128)(2,1)S(1)} %fusion.49) | copy-start | bytes 786436
  773.0 102.4 %all-gather.9.cloned.1.call-start = ((), (), s32[]{:S(2)}) async-start(), calls=%async_computation.7 | async-start | bytes 2162688 | tf_op jit(solution)/shard_map/all_gather | solution.py:133
  773.2 115.0 %copy-start.8 = (bf16[1,1,256,128]{2,3,1,0:T(8,128)(2,1)}, bf16[1,1,256,128]{2,3,1,0:T(8,128)(2,1)S(1)}, u32[]{:S(2)}) copy-start(bf16[1,1,256,128]{2,3,1,0:T(8,128)(2,1)S(1)} %get-tuple-element.108) | copy-start | bytes 196612
  773.3 115.1 %copy-start.10 = (bf16[1,1,256,128]{2,3,1,0:T(8,128)(2,1)}, bf16[1,1,256,128]{2,3,1,0:T(8,128)(2,1)S(1)}, u32[]{:S(2)}) copy-start(bf16[1,1,256,128]{2,3,1,0:T(8,128)(2,1)S(1)} %get-tuple-element.109) | copy-start | bytes 196612
  773.3 115.3 %copy-start.12 = (bf16[1,1,256,128]{2,3,1,0:T(8,128)(2,1)}, bf16[1,1,256,128]{2,3,1,0:T(8,128)(2,1)S(1)}, u32[]{:S(2)}) copy-start(bf16[1,1,256,128]{2,3,1,0:T(8,128)(2,1)S(1)} %get-tuple-element.110) | copy-start | bytes 196612
  773.3 115.4 %copy-start.14 = (bf16[1,1,256,128]{2,3,1,0:T(8,128)(2,1)}, bf16[1,1,256,128]{2,3,1,0:T(8,128)(2,1)S(1)}, u32[]{:S(2)}) copy-start(bf16[1,1,256,128]{2,3,1,0:T(8,128)(2,1)S(1)} %get-tuple-element.111) | copy-start | bytes 196612
  773.3 121.6 %copy-start.6 = (bf16[1,1,256,128]{2,3,1,0:T(8,128)(2,1)}, bf16[1,1,256,128]{2,3,1,0:T(8,128)(2,1)S(1)}, u32[]{:S(2)}) copy-start(bf16[1,1,256,128]{2,3,1,0:T(8,128)(2,1)S(1)} %get-tuple-element.107) | copy-start | bytes 196612
  775.2 48.8 %copy-start.27 = (f32[256,128]{1,0:T(8,128)}, f32[256,128]{1,0:T(8,128)S(1)}, u32[]{:S(2)}) copy-start(f32[256,128]{1,0:T(8,128)S(1)} %copy.732) | copy-start | bytes 393220
  824.3 5.0 collective-permute-start.6
  830.0 110.1 %all-gather.11.cloned.1.call-start = ((), (), s32[]{:S(2)}) async-start(), calls=%async_computation.8 | async-start | bytes 2162688 | tf_op jit(solution)/shard_map/all_gather | solution.py:133
  832.4 43.0 %copy-start.29 = (f32[256,128]{1,0:T(8,128)}, f32[256,128]{1,0:T(8,128)S(1)}, u32[]{:S(2)}) copy-start(f32[256,128]{1,0:T(8,128)S(1)} %copy.742) | copy-start | bytes 393220
  880.1 5.0 collective-permute-start.7
  885.8 111.2 %all-gather.13.cloned.1.call-start = ((), (), s32[]{:S(2)}) async-start(), calls=%async_computation.9 | async-start | bytes 2162688 | tf_op jit(solution)/shard_map/all_gather | solution.py:133
  890.3 49.7 %copy-start.21 = (f32[256,128]{1,0:T(8,128)}, f32[256,128]{1,0:T(8,128)S(1)}, u32[]{:S(2)}) copy-start(f32[256,128]{1,0:T(8,128)S(1)} %copy.754) | copy-start | bytes 393220
  944.8 5.0 collective-permute-start.8
  950.5 102.6 %all-gather.15.cloned.1.call-start = ((), (), s32[]{:S(2)}) async-start(), calls=%async_computation.10 | async-start | bytes 2162688 | tf_op jit(solution)/shard_map/all_gather | solution.py:133
  1002.0 5.0 collective-permute-start.9
  1007.7 101.3 %all-gather.17.cloned.1.call-start = ((), (), s32[]{:S(2)}) async-start(), calls=%async_computation.11 | async-start | bytes 2162688 | tf_op jit(solution)/shard_map/all_gather | solution.py:133
  1007.7 45.3 %copy-start.25 = (f32[256,128]{1,0:T(8,128)S(1)}, f32[256,128]{1,0:T(8,128)}, u32[]{:S(2)}) copy-start(f32[256,128]{1,0:T(8,128)} %copy.778) | copy-start | bytes 393220
  1009.7 45.6 %copy-start.30 = (f32[1,9,64,128]{3,2,1,0:T(8,128)}, f32[1,9,64,128]{3,2,1,0:T(8,128)S(1)}, u32[]{:S(2)}) copy-start(f32[1,9,64,128]{3,2,1,0:T(8,128)S(1)} %constant_dynamic-update-slice_fusion.18) | copy-start | bytes 884740
  1057.9 5.0 collective-permute-start.10
  1063.6 107.8 %all-gather.19.cloned.1.call-start = ((), (), s32[]{:S(2)}) async-start(), calls=%async_computation.12 | async-start | bytes 2162688 | tf_op jit(solution)/shard_map/all_gather | solution.py:133
  1120.3 5.0 collective-permute-start.11
  1133.6 27.4 %copy-start.24 = (f32[256,128]{1,0:T(8,128)S(1)}, f32[256,128]{1,0:T(8,128)}, u32[]{:S(2)}) copy-start(f32[256,128]{1,0:T(8,128)} %copy.790) | copy-start | bytes 393220
  1164.6 27.1 %copy-start.41 = (bf16[256,128]{0,1:T(8,128)(2,1)S(1)}, bf16[256,128]{0,1:T(8,128)(2,1)}, u32[]{:S(2)}) copy-start(bf16[256,128]{0,1:T(8,128)(2,1)} %copy.930) | copy-start | bytes 196612
  1164.6 27.4 %copy-start.40 = (bf16[256,128]{0,1:T(8,128)(2,1)S(1)}, bf16[256,128]{0,1:T(8,128)(2,1)}, u32[]{:S(2)}) copy-start(bf16[256,128]{0,1:T(8,128)(2,1)} %copy.929) | copy-start | bytes 196612
  (60 other events, 379.0 us)
Sparse Core Ops, SparseCore 0:
  14.7 80.2 reduce-scatter.21
  107.3 79.8 reduce-scatter.23
  199.5 79.7 reduce-scatter.25
  291.6 79.8 reduce-scatter.27
  383.8 79.7 reduce-scatter.29
  475.9 79.7 reduce-scatter.31
  568.1 79.6 reduce-scatter.33
  773.1 46.3 all-gather.20
  830.1 45.2 all-gather.8
  885.9 45.2 all-gather.10
  950.6 46.3 all-gather.12
  1007.8 45.2 all-gather.14
  1063.7 45.2 all-gather.16
  1126.1 45.2 all-gather.18
where the time goes:
time: 1230 us; the launch traced here: 1210 us
  waiting for transfers between devices  730 us (59%)
  local copies, waits for them, and re-layouts  175 us (14%)
  matrix products  124 us (10%)
  blocking collectives  121 us (10%)
  starting transfers between devices  28.8 us (2%)
  other arithmetic  18.1 us (1%)
  between operations  17.3 us (1%)
    unnamed x21, waiting for transfers between devices  554 us
    all_gather x7, waiting for transfers between devices, local(): lax.all_gather(back, 'chan', axis=1, tiled=True)  152 us
    psum x1, blocking collectives, local(): lax.psum(jnp.dot(state, head_weight, preferred_element_type=jnp.float32),...  121 us
    unnamed x234, local copies, waits for them, and re-layouts  71.9 us
    another operation x70, local copies, waits for them, and re-layouts, kernel_grad(): return jnp.stack(pieces)  44.8 us
    dot_general x63, matrix products, kernel_grad(): jnp.einsum('tgi,tgo->igo', shifted, grads3, preferred_element_type=jnp.fl...  41.1 us
    conv_general_dilated x20, matrix products, conv_local(): lax.conv_general_dilated(field[None], kernel, (1,), [(half, half)], dimen...  37 us
    slice x63, local copies, waits for them, and re-layouts, kernel_grad(): shifted = padded[k:k + steps].reshape(steps, chans // width, width)  36 us
  transfers between devices with their start and end apart: 26, of which 25 were waited for; matrix products, arithmetic and copies ran while one was open for 15% of the time, Pallas kernels for 0%

commit v1 on v0

v1 whole, which is shorter than its diff:
```python
import jax
import jax.numpy as jnp
from jax import lax
from jax.experimental import pallas as pl
from jax.experimental.pallas import tpu as pltpu
from jax.sharding import PartitionSpec as P

CLASSES = 3
LOSS_SCALE = 2048
NX, NY, NC, NZ = 4, 4, 2, 4
LIVE = 3
F32, BF16 = jnp.float32, jnp.bfloat16
HIGH = lax.Precision.HIGHEST
MESH = pl.DeviceIdType.MESH


def nn(a, b, precision=None):
    return lax.dot_general(a, b, (((1,), (0,)), ((), ())), precision=precision, preferred_element_type=F32)


def nt(a, b, precision=None):
    return lax.dot_general(a, b, (((1,), (1,)), ((), ())), precision=precision, preferred_element_type=F32)


def tn(a, b, precision=None):
    return lax.dot_general(a, b, (((0,), (0,)), ((), ())), precision=precision, preferred_element_type=F32)


def wait_bytes(ref, sem):
    pltpu.make_async_copy(ref, ref, sem).wait()


def kernel(
    inputs, labels, cw, pw, head,
    out_gp, out_gc,
    w_all, cw_all, dense, cols, conv_out, act, state, pad, cgrad,
    psend, precv, summed, r1a, r1b, s1a, s1b, r2a, r2b,
    gathered, gsend, gnear, grecv, frecv, gcsend, gcrecv,
    heads, w3h, tsend, trecv, score_own, score_in,
    send, recv, cw_sem, w_sem,
):
    steps, width = inputs.shape[1], inputs.shape[2]
    taps, group = cw.shape[1], cw.shape[2]
    half = taps // 2
    top_rows = steps // 2
    span = NY * NC * width
    rows_a, rows_b = pl.ds(0, top_rows), pl.ds(top_rows, top_rows)
    z = lax.axis_index("section")
    me = lax.axis_index("chan")
    c = lax.rem(me, NC)
    y = lax.rem(lax.div(me, NC), NY)
    x = lax.div(me, NC * NY)
    other = 1 - c
    sibling = {"chan": me + 1 - 2 * c}
    xs = [lax.rem(x + 1 + r, NX) for r in range(NX)]
    ys = [lax.rem(y + 1 + r, NY) for r in range(NY)]
    xl = [lax.rem(x + NX - 1 - r, NX) for r in range(NX)]
    yl = [lax.rem(y + NY - 1 - r, NY) for r in range(NY)]
    at_x = [{"chan": (xs[r] * NY + y) * NC + c} for r in range(NX - 1)]
    at_y = [{"chan": (x * NY + ys[r]) * NC + c} for r in range(NY - 1)]
    zs = [lax.rem(z + 1 + r, NZ) for r in range(NZ - 1)]
    up, down = {"section": zs[0]}, {"section": zs[2]}

    count = [0]
    sent = []

    def link(src, dst, device, when=None):
        n = count[0]
        count[0] += 1
        copy = pltpu.make_async_remote_copy(
            src_ref=src, dst_ref=dst, send_sem=send.at[n], recv_sem=recv.at[n],
            device_id=device, device_id_type=MESH,
        )
        sent.append((copy, when))
        return copy

    barrier = pltpu.get_barrier_semaphore()
    peers = [sibling] + at_x + at_y + [{"section": s} for s in zs]
    for peer in peers:
        pl.semaphore_signal(barrier, inc=1, device_id=peer, device_id_type=MESH)
    pl.semaphore_wait(barrier, len(peers))

    pltpu.make_async_copy(cw.at[0], cw_all.at[z], cw_sem.at[z]).start()
    for r in range(NZ - 1):
        n = count[0]
        count[0] += 1
        copy = pltpu.make_async_remote_copy(
            src_ref=cw.at[0], dst_ref=cw_all.at[z], send_sem=send.at[n], recv_sem=cw_sem.at[z],
            device_id={"section": zs[r]}, device_id_type=MESH,
        )
        copy.start()
        sent.append((copy, None))

    def w_cols(r):
        return pl.ds(pl.multiple_of(xs[r] * span, span), span)

    w_local, w_up, w_down, w_far = {}, {}, {}, {}

    def w_copy(src, b, r, device, when):
        n = count[0]
        count[0] += 1
        copy = pltpu.make_async_remote_copy(
            src_ref=src, dst_ref=w_all.at[b, :, w_cols(r)], send_sem=send.at[n], recv_sem=w_sem.at[b, r],
            device_id=device, device_id_type=MESH,
        )
        sent.append((copy, when))
        return copy

    for b in range(LIVE):
        home = z == b
        relays = [z == (b + 1) % NZ, z == (b + 3) % NZ]
        for r in range(NX):
            src = pw.at[0, :, w_cols(r)]
            w_local[b, r] = pltpu.make_async_copy(src, w_all.at[b, :, w_cols(r)], w_sem.at[b, r])
            w_up[b, r] = w_copy(src, b, r, up, home)
            w_down[b, r] = w_copy(src, b, r, down, home)
            w_far[b, r] = w_copy(
                w_all.at[b, :, w_cols(r)], b, r, [up, down][r % 2], relays[r % 2]
            )

    def w_launch(b, r):
        @pl.when(z == b)
        def _():
            w_up[b, r].start()
            w_down[b, r].start()
            w_local[b, r].start()

    def w_arrive(b, r):
        wait_bytes(w_all.at[b, :, w_cols(r)], w_sem.at[b, r])

        @pl.when(z == [(b + 1) % NZ, (b + 3) % NZ][r % 2])
        def _():
            w_far[b, r].start()

    for r in range(NX):
        w_launch(0, r)

    last = z == NZ - 1
    head_core = link(heads.at[x, y, c], heads.at[x, y, c], sibling, last)
    head_x = [link(heads.at[x, y], heads.at[x, y], at_x[r], last) for r in range(NX - 1)]
    head_y = [link(heads.at[:, y], heads.at[:, y], at_y[r], last) for r in range(NY - 1)]
    w3h_out = [link(w3h, w3h, {"section": zs[r]}, last) for r in range(NZ - 1)]

    @pl.when(last)
    def _():
        heads[x, y, c] = head[...]
        head_core.start()
        head_core.wait_recv()
        for copy in head_x:
            copy.start()
        for copy in head_x:
            copy.wait_recv()
        for copy in head_y:
            copy.start()
        for copy in head_y:
            copy.wait_recv()

        def fold(i, total):
            whole = jnp.concatenate(
                [heads[i, j, k] for j in range(NY) for k in range(NC)], axis=1
            ).astype(BF16)
            return total + nt(whole, pw[0, :, pl.ds(pl.multiple_of(i * span, span), span)])

        w3h[...] = lax.fori_loop(0, NX, fold, jnp.zeros(w3h.shape, F32))
        for copy in w3h_out:
            copy.start()

    lane = lax.broadcasted_iota(jnp.int32, (group, width), 1)
    first_group = lane < group
    edge = 8
    pad[pl.ds(0, edge), :] = jnp.zeros((edge, width), F32)
    pad[pl.ds(edge + steps, edge), :] = jnp.zeros((edge, width), F32)
    state[...] = inputs[z].astype(F32)

    def conv(b):
        wait_bytes(cw_all.at[b], cw_sem.at[b])
        for k in range(taps):
            tap = cw_all[b, k].astype(F32)
            dense[b, pl.ds(k * width, group), :] = jnp.where(first_group, tap, 0.0).astype(BF16)
            dense[b, pl.ds(k * width + group, group), :] = jnp.where(first_group, 0.0, tap).astype(BF16)
        pad[pl.ds(edge, steps), :] = state[...]
        for k in range(taps):
            cols[b, :, pl.ds(k * width, width)] = pad[pl.ds(edge + k - half, steps), :].astype(BF16)
        value = nn(cols[b], dense[b])
        conv_out[b] = value
        act[b] = (value * jax.nn.sigmoid(value)).astype(BF16)

    def piece_cols(b, xr, core):
        return jnp.concatenate(
            [
                w_all[b, :, pl.ds(pl.multiple_of(xr * span + (j * NC + core) * width, width), width)]
                for j in range(NY)
            ],
            axis=1,
        )

    def mix(b):
        to_core = [link(psend.at[b, xs[r]], precv.at[b, xs[r]], sibling) for r in range(NX)]
        a1 = [link(summed.at[b, xs[r], :, rows_a], r1a.at[b, r], at_x[r]) for r in range(NX - 1)]
        b1 = [link(summed.at[b, :, ys[r], rows_b], r1b.at[b, r], at_y[r]) for r in range(NY - 1)]
        a2 = [link(s1a.at[b, ys[r]], r2a.at[b, r], at_y[r]) for r in range(NY - 1)]
        b2 = [link(s1b.at[b, xs[r]], r2b.at[b, r], at_x[r]) for r in range(NX - 1)]
        for r in range(NX + 1):
            if r < NX:
                w_arrive(b, r)
                if b == 0:
                    w_launch(1, r)
                part = nn(act[b], piece_cols(b, xs[r], other))
                for j in range(NY):
                    psend[b, xs[r], j] = part[:, j * width : (j + 1) * width].astype(BF16)
                to_core[r].start()
            if r >= 1:
                part = nn(act[b], piece_cols(b, xs[r - 1], c))
                to_core[r - 1].wait_recv()
                for j in range(NY):
                    summed[b, xs[r - 1], j] = (
                        part[:, j * width : (j + 1) * width] + precv[b, xs[r - 1], j].astype(F32)
                    ).astype(BF16)
                if r < NX:
                    a1[r - 1].start()
        for copy in b1:
            copy.start()
        if b == 0:
            for r in range(NX):
                w_launch(2, r)
        for copy in a1:
            copy.wait_recv()
        for j in range(NY):
            total = summed[b, x, j, rows_a].astype(F32)
            for r in range(NX - 1):
                total = total + r1a[b, r, j].astype(F32)
            s1a[b, j] = total.astype(BF16)
        for copy in a2:
            copy.start()
        for copy in b1:
            copy.wait_recv()
        for i in range(NX):
            total = summed[b, i, y, rows_b].astype(F32)
            for r in range(NY - 1):
                total = total + r1b[b, r, i].astype(F32)
            s1b[b, i] = total.astype(BF16)
        for copy in b2:
            copy.start()
        for copy in a2:
            copy.wait_recv()
        total = s1a[b, y].astype(F32)
        for r in range(NY - 1):
            total = total + r2a[b, r].astype(F32)
        state[rows_a, :] = (state[rows_a, :] + total).astype(BF16).astype(F32)
        for copy in b2:
            copy.wait_recv()
        total = s1b[b, x].astype(F32)
        for r in range(NX - 1):
            total = total + r2b[b, r].astype(F32)
        state[rows_b, :] = (state[rows_b, :] + total).astype(BF16).astype(F32)

    for b in range(LIVE):
        conv(b)
        mix(b)
    conv(LIVE)

    s_core = link(score_own.at[0], score_in.at[0], sibling)
    s_x = [link(score_own.at[1], score_in.at[1 + r], at_x[r]) for r in range(NX - 1)]
    s_y = [link(score_own.at[2], score_in.at[NX + r], at_y[r]) for r in range(NY - 1)]

    @pl.when(z != NZ - 1)
    def _():
        for r in range(NZ - 1):
            @pl.when(zs[NZ - 2 - r] == NZ - 1)
            def _():
                w3h_out[r].wait_recv()

    scores = nt(head[...], state[...], HIGH) + nt(w3h[...], act[LIVE].astype(F32), HIGH)
    score_own[0] = scores
    s_core.start()
    s_core.wait_recv()
    scores = scores + score_in[0]
    score_own[1] = scores
    for copy in s_x:
        copy.start()
    for copy in s_x:
        copy.wait_recv()
    for r in range(NX - 1):
        scores = scores + score_in[1 + r]
    score_own[2] = scores
    for copy in s_y:
        copy.start()
    for copy in s_y:
        copy.wait_recv()
    for r in range(NY - 1):
        scores = scores + score_in[NX + r]
    classes = lax.broadcasted_iota(jnp.int32, scores.shape, 0)
    hot = (classes == labels[pl.ds(z, 1), :]).astype(F32)
    top = (jax.nn.sigmoid(scores) - hot) * (LOSS_SCALE / (inputs.shape[0] * steps))
    top_t = top.T
    back = nn(top_t, head[...], HIGH).astype(BF16).astype(F32)
    act_grad = nn(top_t, w3h[...], HIGH)

    def silu_grad(b, act_grad):
        value = conv_out[b]
        s = jax.nn.sigmoid(value)
        result = (act_grad * s * (1.0 + value * (1.0 - s))).astype(BF16)
        cgrad[b] = result
        return result

    def input_grad(b):
        pad[pl.ds(edge, steps), :] = cgrad[b].astype(F32)
        total = jnp.zeros((steps, width), F32)
        for k in range(taps):
            shifted = pad[pl.ds(edge - k + half, steps), :].astype(BF16)
            total = total + nt(shifted, dense[b, pl.ds(k * width, width), :])
        return total

    def conv_weight_grad(b):
        whole = tn(cols[b], cgrad[b])
        n = count[0]
        count[0] += NZ - 1
        copies = []
        for d in range(1, NZ):
            copy = pltpu.make_async_remote_copy(
                src_ref=gcsend.at[b], dst_ref=gcrecv.at[d - 1], send_sem=send.at[n + d - 1],
                recv_sem=recv.at[gc_recv + d - 1], device_id={"section": jnp.int32(b)}, device_id_type=MESH,
            )
            sent.append((copy, z == (b + d) % NZ))
            copies.append(copy)
        for k in range(taps):
            piece = jnp.where(
                first_group,
                whole[k * width : k * width + group],
                whole[k * width + group : (k + 1) * width],
            )

            @pl.when(z == b)
            def _():
                out_gc[0, k] = piece

            @pl.when(z != b)
            def _():
                gcsend[b, k] = piece.astype(BF16)

        for d in range(1, NZ):
            @pl.when(z == (b + d) % NZ)
            def _():
                copies[d - 1].start()

    gc_recv = count[0]
    count[0] += NZ - 1

    gp_recv_n = count[0]
    count[0] += 2 * NX
    far_recv_n = count[0]
    count[0] += 2 * NX

    def span_at(i):
        return pl.ds(i * span, span)

    def gather_links(b):
        own = gathered.at[b, x, y, c]
        links = {}
        links["a1"] = [
            link(own.at[rows_a], own.at[rows_a], at_y[r]) for r in range(NY - 1)
        ]
        links["b1"] = [
            link(own.at[rows_b], own.at[rows_b], at_x[r]) for r in range(NX - 1)
        ]
        group_a = gathered.at[b, x, :, c, rows_a]
        group_b = gathered.at[b, :, y, c, rows_b]
        links["a2"] = [link(group_a, group_a, at_x[r]) for r in range(NX - 1)]
        links["b2"] = [link(group_b, group_b, at_y[r]) for r in range(NY - 1)]
        ca, cb = [link(group_a, group_a, sibling)], [link(group_b, group_b, sibling)]
        for r in range(NX - 1):
            part = gathered.at[b, xl[r], :, c, rows_a]
            ca.append(link(part, part, sibling))
        for r in range(NY - 1):
            part = gathered.at[b, :, yl[r], c, rows_b]
            cb.append(link(part, part, sibling))
        links["ca"], links["cb"] = ca, cb
        return links

    def gather_start(b, links):
        gathered[b, x, y, c] = back_state[0].astype(BF16)
        for copy in links["a1"] + links["b1"]:
            copy.start()

    def gather_second(links):
        for copy in links["a1"]:
            copy.wait_recv()
        for copy in links["a2"] + links["ca"][:1]:
            copy.start()
        for copy in links["b1"]:
            copy.wait_recv()
        for copy in links["b2"] + links["cb"][:1]:
            copy.start()

    def gather_last(links):
        for r in range(NX - 1):
            links["a2"][r].wait_recv()
            links["ca"][1 + r].start()
            links["b2"][r].wait_recv()
            links["cb"][1 + r].start()
        for copy in links["ca"] + links["cb"]:
            copy.wait_recv()

    def piece_of(b, i):
        return jnp.concatenate([gathered[b, i, j, k] for j in range(NY) for k in range(NC)], axis=1)

    def act_grad_of(b):
        def step(i, total):
            return total + nt(piece_of(b, i), w_all[b, :, pl.ds(pl.multiple_of(i * span, span), span)])

        return lax.fori_loop(0, NX, step, jnp.zeros((steps, width), F32))

    def point_links(b):
        home = {"section": jnp.int32(b)}
        links = {"near": [[], []], "far": []}
        for side, near in enumerate([(b + 1) % NZ, (b + 3) % NZ]):
            for i in range(NX):
                n = count[0]
                count[0] += 1
                copy = pltpu.make_async_remote_copy(
                    src_ref=gsend.at[b, :, span_at(i)], dst_ref=grecv.at[side, :, span_at(i)],
                    send_sem=send.at[n], recv_sem=recv.at[gp_recv_n + side * NX + i],
                    device_id=home, device_id_type=MESH,
                )
                sent.append((copy, z == near))
                links["near"][side].append(copy)
        for i in range(NX):
            n = count[0]
            count[0] += 1
            side = i % 2
            copy = pltpu.make_async_remote_copy(
                src_ref=gsend.at[b, :, span_at(i)], dst_ref=frecv.at[side, i // 2],
                send_sem=send.at[n], recv_sem=recv.at[far_recv_n + i],
                device_id={"section": jnp.int32([(b + 1) % NZ, (b + 3) % NZ][side])}, device_id_type=MESH,
            )
            sent.append((copy, z == (b + 2) % NZ))
            links["far"].append(copy)
        return links

    def point_grad(b, links):
        act_t = act[b].astype(F32).T.astype(BF16)

        def chunk(i):
            return nn(act_t, piece_of(b, i))

        @pl.when(z == b)
        def _():
            for i in range(NX):
                out_gp[0, :, span_at(i)] = chunk(i)

        @pl.when(z == (b + 2) % NZ)
        def _():
            for i in range(NX):
                gsend[b, :, span_at(i)] = chunk(i).astype(BF16)
                links["far"][i].start()

        for side in range(2):
            @pl.when(z == [(b + 1) % NZ, (b + 3) % NZ][side])
            def _():
                for i in range(1 - side, NX, 2):
                    gsend[b, :, span_at(i)] = chunk(i).astype(BF16)
                    links["near"][side][i].start()
                for i in range(side, NX, 2):
                    gnear[i // 2] = chunk(i)

    def point_relay(b, links):
        for side in range(2):
            @pl.when(z == [(b + 1) % NZ, (b + 3) % NZ][side])
            def _():
                for i in range(side, NX, 2):
                    links["far"][i].wait_recv()
                    gsend[b, :, span_at(i)] = (gnear[i // 2] + frecv[side, i // 2].astype(F32)).astype(BF16)
                    links["near"][side][i].start()

    back_state = [back]
    silu_grad(LIVE, act_grad)
    back_state[0] = (back_state[0] + input_grad(LIVE)).astype(BF16).astype(F32)
    links = gather_links(LIVE - 1)
    gather_start(LIVE - 1, links)
    folded = nn(top, act[LIVE].astype(F32), HIGH)
    t_links = []
    for d in range(1, NZ):
        copy = link(tsend, trecv.at[d - 1], {"section": jnp.int32(NZ - 1)}, z == (NZ - 1 + d) % NZ)
        t_links.append(copy)
    tsend[...] = folded
    for d in range(1, NZ):
        @pl.when(z == (NZ - 1 + d) % NZ)
        def _():
            t_links[d - 1].start()

    gather_second(links)
    conv_weight_grad(LIVE)
    pending = None
    for b in range(LIVE - 1, -1, -1):
        if pending is not None:
            point_relay(*pending)
        gather_last(links)
        silu_grad(b, act_grad_of(b))
        if b > 0:
            back_state[0] = (back_state[0] + input_grad(b)).astype(BF16).astype(F32)
            links = gather_links(b - 1)
            gather_start(b - 1, links)
        p_links = point_links(b)
        point_grad(b, p_links)
        if b > 0:
            gather_second(links)
        conv_weight_grad(b)
        pending = (b, p_links)
    point_relay(*pending)

    @pl.when(last)
    def _():
        total = tsend[...]
        for d in range(1, NZ):
            t_links[d - 1].wait_recv()
            total = total + trecv[d - 1]
        total_t = total.T
        for i in range(NX):
            whole = jnp.concatenate([heads[i, j, k] for j in range(NY) for k in range(NC)], axis=1)
            out_gp[0, :, span_at(i)] = nn(total_t, whole, HIGH)

    for d in range(1, NZ):
        wait_bytes(gcrecv.at[d - 1], recv.at[gc_recv + d - 1])
    for k in range(taps):
        total = out_gc[0, k]
        for d in range(1, NZ):
            total = total + gcrecv[d - 1, k].astype(F32)
        out_gc[0, k] = total

    @pl.when(z != NZ - 1)
    def _():
        for i in range(NX):
            for side in ((1, 0) if i % 2 == 0 else (0, 1)):
                wait_bytes(grecv.at[side, :, span_at(i)], recv.at[gp_recv_n + side * NX + i])
            out_gp[0, :, span_at(i)] = (
                out_gp[0, :, span_at(i)]
                + grecv[0, :, span_at(i)].astype(F32)
                + grecv[1, :, span_at(i)].astype(F32)
            )

    for copy, when in sent:
        if when is None:
            copy.wait_send()
        else:
            pl.when(when)(copy.wait_send)
    assert count[0] <= send.shape[0], count[0]


def local(inputs, labels, conv_weight, point_weight, head_weight):
    micro, steps, width = inputs.shape
    blocks, taps, group, _ = conv_weight.shape
    all_blocks = blocks * lax.axis_size("section")
    chans = point_weight.shape[2]
    span = chans // NX
    part = width
    half = steps // 2
    head = jnp.pad(head_weight.astype(F32).T, ((0, 8 - CLASSES), (0, 0)))
    vmem = pl.BlockSpec(memory_space=pltpu.VMEM)
    V = pltpu.VMEM
    scratch = [
        V((LIVE, width, chans), BF16),
        V((all_blocks, taps, group, width), BF16),
        V((all_blocks, taps * width, width), BF16),
        V((all_blocks, steps, taps * width), BF16),
        V((all_blocks, steps, width), F32),
        V((all_blocks, steps, width), BF16),
        V((steps, width), F32),
        V((steps + 16, width), F32),
        V((all_blocks, steps, width), BF16),
        V((LIVE, NX, NY, steps, part), BF16),
        V((LIVE, NX, NY, steps, part), BF16),
        V((LIVE, NX, NY, steps, part), BF16),
        V((LIVE, NX - 1, NY, half, part), BF16),
        V((LIVE, NY - 1, NX, half, part), BF16),
        V((LIVE, NY, half, part), BF16),
        V((LIVE, NX, half, part), BF16),
        V((LIVE, NY - 1, half, part), BF16),
        V((LIVE, NX - 1, half, part), BF16),
        V((LIVE, NX, NY, NC, steps, part), BF16),
        V((LIVE, width, chans), BF16),
        V((2, width, span), F32),
        V((2, width, chans), BF16),
        V((2, 2, width, span), BF16),
        V((all_blocks, taps, group, width), BF16),
        V((NZ - 1, taps, group, width), BF16),
        V((NX, NY, NC, 8, width), F32),
        V((8, width), F32),
        V((8, width), F32),
        V((NZ - 1, 8, width), F32),
        V((3, 8, steps), F32),
        V((NX + NY - 1, 8, steps), F32),
        pltpu.SemaphoreType.DMA((320,)),
        pltpu.SemaphoreType.DMA((320,)),
        pltpu.SemaphoreType.DMA((all_blocks,)),
        pltpu.SemaphoreType.DMA((LIVE, NX)),
    ]
    return pl.pallas_call(
        kernel,
        out_shape=(
            jax.ShapeDtypeStruct(point_weight.shape, F32),
            jax.ShapeDtypeStruct(conv_weight.shape, F32),
        ),
        in_specs=[vmem] * 5,
        out_specs=(vmem, vmem),
        scratch_shapes=scratch,
        compiler_params=pltpu.CompilerParams(
            collective_id=0, has_side_effects=True, vmem_limit_bytes=58 * 1024 * 1024
        ),
    )(inputs, labels, conv_weight, point_weight, head)


def solution(mesh):
    placed = (
        P(None, None, "chan"),
        P(),
        P("section", None, None, "chan"),
        P("section", "chan", None),
        P("chan", None),
    )
    return jax.shard_map(
        local,
        mesh=mesh,
        in_specs=placed,
        out_specs=(P("section", "chan", None), P("section", None, None, "chan")),
        check_vma=False,
    )
```

time: 1230 us -> 226 us (0.18); the launches traced: 1210 us -> 226 us
  waiting for transfers between devices: 730 us -> 0 us
  Pallas kernels: 0 us -> 220 us
  local copies, waits for them, and re-layouts: 175 us -> 3.87 us
  matrix products: 124 us -> 0 us
  blocking collectives: 121 us -> 0 us
  starting transfers between devices: 28.8 us -> 0 us
  other arithmetic: 18.1 us -> 1.28 us
  between operations: 17.3 us -> 0.65 us
    unnamed x21 -> x0, waiting for transfers between devices: 554 us -> none
    pallas_call x0 -> x1, Pallas kernels: none -> 220 us  [local(): pl.pallas_call(kernel, out_shape=(jax.ShapeDtypeStruct(point_weight.shape...]
    all_gather x7 -> x0, waiting for transfers between devices: 152 us -> none  [local(): lax.all_gather(back, 'chan', axis=1, tiled=True)]
    psum x1 -> x0, blocking collectives: 121 us -> none  [local(): lax.psum(jnp.dot(state, head_weight, preferred_element_type=jnp.float32),...]
    dot_general x98 -> x0, matrix products: 87.4 us -> none  [the longest x63 41.1 us: kernel_grad(): jnp.einsum('tgi,tgo->igo', shifted, grads3, preferred_element_type=jnp.fl...]
    unnamed x234 -> x4, local copies, waits for them, and re-layouts: 71.9 us -> 3.87 us
    another operation x72 -> x0, local copies, waits for them, and re-layouts: 44.9 us -> none  [the longest x70 44.8 us: kernel_grad(): return jnp.stack(pieces)]
    conv_general_dilated x20 -> x0, matrix products: 37 us -> none  [conv_local(): lax.conv_general_dilated(field[None], kernel, (1,), [(half, half)], dimen...]
  transfers between devices with their start and end apart: 26 -> 0, of which waited for: 25 -> 0; matrix products, arithmetic and copies ran while one was open for 15% -> 0% of each run, Pallas kernels for 0% -> 0%
where the time goes in v1:
time: 226 us
  Pallas kernels  220 us (97%)
  local copies, waits for them, and re-layouts  3.87 us (2%)
    pallas_call x1, Pallas kernels, local(): pl.pallas_call(kernel, out_shape=(jax.ShapeDtypeStruct(point_weight.shape...  220 us

profile of v1, /device:TPU:1, one launch (start us, length us, event | category | flops | bytes accessed | tf_op | source)
XLA Modules:
  0.0 225.6 jit_solution(399926330805993977)
XLA Ops:
  0.6 1.3 pad_convert_fusion.head
  1.9 219.9 %shard_map.68 = (f32[1,128,4096]{2,1,0:T(8,128)}, f32[1,9,64,128]{3,2,1,0:T(8,128)}) custom-call(bf16[4,256,128]{2,1,0:T(8,128)(2,1)} %inputs.1, s32[4,256]{1,0:T(4,128)} %labels.1, bf16[1,9,64,128]{3,2,1,0:T(8,128)(2,1)} %cw.1, bf16[1,128,4096]{2,1,0:T(8,128)(2,1)} %pw.1, f32[8,128]{1,0:T(8,128)} %pad_convert_fusion.head), custom_call_target="tpu_custom_call" | custom-call | tf_op jit(solution)/shard_map/pallas_call | solution.py:597
  221.8 0.0 copy-start
  221.8 3.2 %copy.9 = f32[1,128,4096]{2,1,0:T(8,128)} copy(f32[1,128,4096]{2,1,0:T(8,128)} %get-tuple-element.4) | data formatting | bytes 4194304
  224.9 0.0 copy-done
  224.9 0.7 copy.10
Async XLA Ops:
  221.8 3.2 %copy-start = (f32[1,9,64,128]{3,2,1,0:T(8,128)S(1)}, f32[1,9,64,128]{3,2,1,0:T(8,128)}, u32[]{:S(2)}) copy-start(f32[1,9,64,128]{3,2,1,0:T(8,128)} %get-tuple-element.5) | copy-start | bytes 884740

commit v2 on v0

v2 whole, which is shorter than its diff:
```python
import jax
import jax.numpy as jnp
from jax import lax
from jax.experimental import pallas as pl
from jax.experimental.pallas import tpu as pltpu
from jax.sharding import PartitionSpec as P

CLASSES = 3
LOSS_SCALE = 2048
NX, NY, NC, NZ = 4, 4, 2, 4
LIVE = 3
SUB = 4
F32, BF16 = jnp.float32, jnp.bfloat16
HIGH = lax.Precision.HIGHEST
MESH = pl.DeviceIdType.MESH


def nn(a, b, precision=None):
    return lax.dot_general(a, b, (((1,), (0,)), ((), ())), precision=precision, preferred_element_type=F32)


def nt(a, b, precision=None):
    return lax.dot_general(a, b, (((1,), (1,)), ((), ())), precision=precision, preferred_element_type=F32)


def tn(a, b, precision=None):
    return lax.dot_general(a, b, (((0,), (0,)), ((), ())), precision=precision, preferred_element_type=F32)


def wait_bytes(ref, sem):
    pltpu.make_async_copy(ref, ref, sem).wait()


def kernel(
    inputs, labels, cw, pw, head,
    out_gp, out_gc,
    w_all, cw_all, w_last, start, dense, cols, conv_out, act, state, pad, cgrad,
    pas, par, pbs, pbr, sa, sb, r1a, r1b, s1a, s1b, r2a, r2b,
    ga, gb, gsend, crecv, gpart, ghome, gcsend, gccrecv, gcpart,
    heads, w3h, tsend, trecv, score_own, score_in,
    send, recv, gp_send, gp_recv, gc_send, gc_recv, local_sem, out_sem,
):
    steps, width = start.shape
    taps, group = cw.shape[1], cw.shape[2]
    half = taps // 2
    top_rows = steps // 2
    pair = NC * width
    span = NY * pair
    rows_a, rows_b = pl.ds(0, top_rows), pl.ds(top_rows, top_rows)
    z = lax.axis_index("section")
    me = lax.axis_index("chan")
    c = lax.rem(me, NC)
    y = lax.rem(lax.div(me, NC), NY)
    x = lax.div(me, NC * NY)
    other = 1 - c
    sibling = {"chan": me + 1 - 2 * c}
    xs = [lax.rem(x + 1 + r, NX) for r in range(NX)]
    ys = [lax.rem(y + 1 + r, NY) for r in range(NY)]
    xl = [lax.rem(x + NX - 1 - r, NX) for r in range(NX)]
    yl = [lax.rem(y + NY - 1 - r, NY) for r in range(NY)]
    at_x = [{"chan": (xs[r] * NY + y) * NC + c} for r in range(NX - 1)]
    at_y = [{"chan": (x * NY + ys[r]) * NC + c} for r in range(NY - 1)]
    zs = [lax.rem(z + 1 + r, NZ) for r in range(NZ - 1)]
    up, down = {"section": zs[0]}, {"section": zs[2]}
    last = z == NZ - 1

    def is_z(*places):
        hit = z == places[0] % NZ
        for place in places[1:]:
            hit = hit | (z == place % NZ)
        return hit

    count = [0]
    sent = []

    def number():
        count[0] += 1
        return count[0] - 1

    def remote(src, dst, send_sem, recv_sem, device):
        return pltpu.make_async_remote_copy(
            src_ref=src, dst_ref=dst, send_sem=send_sem, recv_sem=recv_sem,
            device_id=device, device_id_type=MESH,
        )

    def link(src, dst, device, when=None):
        n = number()
        copy = remote(src, dst, send.at[n], recv.at[n], device)
        sent.append((copy, when))
        return copy

    pltpu.make_async_copy(inputs.at[z], start, local_sem.at[0]).start()

    @pl.when(last)
    def _():
        pltpu.make_async_copy(pw.at[0], w_last, local_sem.at[1]).start()

    barrier = pltpu.get_barrier_semaphore()
    peers = [sibling] + at_x + at_y + [{"section": s} for s in zs]
    for peer in peers:
        pl.semaphore_signal(barrier, inc=1, device_id=peer, device_id_type=MESH)
    pl.semaphore_wait(barrier, len(peers))

    class Piece:
        def __init__(self, b, way, src, ref):
            n = number()
            self.src, self.ref, self.sem, self.b = src, ref, recv.at[n], b
            device = (up, down)[way]
            order = [b + 1, b + 2, b + 3] if way == 0 else [b + 3, b + 2, b + 1]
            self.relays = is_z(*order[:2])
            self.first = remote(src, ref, send.at[n], recv.at[n], device)
            self.next = remote(ref, ref, send.at[n], recv.at[n], device)
            sent.append((self.next, z != order[2] % NZ))

        def relay(self):
            @pl.when(self.relays)
            def _():
                wait_bytes(self.ref, self.sem)
                self.next.start()

        def ready(self):
            @pl.when(jnp.logical_not(self.relays))
            def _():
                wait_bytes(self.ref, self.sem)

    def broadcast(b):
        ways = []
        for way in range(2):
            kept = pl.ds(0, half + 1) if way == 0 else pl.ds(half + 1, taps - half - 1)
            pieces = [Piece(b, way, cw.at[0, kept], cw_all.at[b, kept])]
            if b < LIVE:
                for r in range(way, NX, 2):
                    for k in range(SUB):
                        size = span // SUB
                        at = pl.ds(pl.multiple_of(xs[r] * span + k * size, size), size)
                        pieces.append(Piece(b, way, pw.at[0, :, at], w_all.at[b, :, at]))
            ways.append(pieces)
        return [piece for both in zip(*ways) for piece in both]

    pieces = [broadcast(b) for b in range(NZ)]

    def launch(b):
        @pl.when(z == b)
        def _():
            for piece in pieces[b]:
                piece.first.start()
            for piece in pieces[b]:
                pltpu.make_async_copy(piece.src, piece.ref, piece.sem).start()

    pumped = [0] * NZ

    def pump(b, amount):
        for piece in pieces[b][pumped[b] : pumped[b] + amount]:
            piece.relay()
        pumped[b] += amount

    head_core = link(heads.at[x, y, c], heads.at[x, y, c], sibling, last)
    head_x = [link(heads.at[x, y], heads.at[x, y], at_x[r], last) for r in range(NX - 1)]
    head_y = [link(heads.at[:, y], heads.at[:, y], at_y[r], last) for r in range(NY - 1)]
    w3h_out = [link(w3h, w3h, {"section": zs[r]}, last) for r in range(NZ - 1)]

    launch(0)

    @pl.when(last)
    def _():
        heads[x, y, c] = head[...]
        head_core.start()

    pump(0, 2)

    @pl.when(last)
    def _():
        head_core.wait_recv()
        for copy in head_x:
            copy.start()

    lane = lax.broadcasted_iota(jnp.int32, (group, width), 1)
    first_group = lane < group
    edge = 8
    pad[pl.ds(0, edge), :] = jnp.zeros((edge, width), F32)
    pad[pl.ds(edge + steps, edge), :] = jnp.zeros((edge, width), F32)
    wait_bytes(start, local_sem.at[0])
    state[...] = start[...].astype(F32)

    def unfold(b):
        pad[pl.ds(edge, steps), :] = state[...]
        for k in range(taps):
            cols[b, :, pl.ds(k * width, width)] = pad[pl.ds(edge + k - half, steps), :].astype(BF16)

    def widen(b):
        for piece in pieces[b][:2]:
            piece.ready()
        for k in range(taps):
            tap = cw_all[b, k].astype(F32)
            dense[b, pl.ds(k * width, group), :] = jnp.where(first_group, tap, 0.0).astype(BF16)
            dense[b, pl.ds(k * width + group, group), :] = jnp.where(first_group, 0.0, tap).astype(BF16)

    def conv(b):
        value = nn(cols[b], dense[b])
        conv_out[b] = value
        act[b] = (value * jax.nn.sigmoid(value)).astype(BF16)

    unfold(0)
    pump(0, len(pieces[0]) // 2)

    @pl.when(last)
    def _():
        for copy in head_x:
            copy.wait_recv()
        for copy in head_y:
            copy.start()

    widen(0)
    conv(0)
    pump(0, len(pieces[0]))
    launch(1)

    def mix(b):
        ca = [link(pas.at[b, r], par.at[b, r], sibling) for r in range(NX)]
        cb = [link(pbs.at[b, r], pbr.at[b, r], sibling) for r in range(NY)]
        a1 = [link(sa.at[b, r], r1a.at[b, r], at_x[r]) for r in range(NX - 1)]
        b1 = [link(sb.at[b, r], r1b.at[b, r], at_y[r]) for r in range(NY - 1)]
        a2 = [link(s1a.at[b, r], r2a.at[b, r], at_y[r]) for r in range(NY - 1)]
        b2 = [link(s1b.at[b, r], r2b.at[b, r], at_x[r]) for r in range(NX - 1)]

        def weights(place, core):
            return jnp.concatenate(
                [
                    w_all[b, :, pl.ds(pl.multiple_of(place(j) * pair + core * width, width), width)]
                    for j in range(NY)
                ],
                axis=1,
            )

        def line_a(r):
            return lambda j: xs[r] * NY + j

        def line_b(r):
            return lambda i: i * NY + ys[r]

        for piece in pieces[b][2:]:
            piece.ready()
        for r in range(NX + 1):
            if r < NX:
                for rows, line, out, copy in ((rows_a, line_a, pas, ca), (rows_b, line_b, pbs, cb)):
                    part = nn(act[b, rows, :], weights(line(r), other))
                    for j in range(NY):
                        out[b, r, j] = part[:, j * width : (j + 1) * width].astype(BF16)
                    copy[r].start()
            if r >= 1:
                q = r - 1
                for rows, line, heard, out, copy, first in (
                    (rows_a, line_a, par, sa, ca, a1),
                    (rows_b, line_b, pbr, sb, cb, b1),
                ):
                    part = nn(act[b, rows, :], weights(line(q), c))
                    copy[q].wait_recv()
                    for j in range(NY):
                        out[b, q, j] = (
                            part[:, j * width : (j + 1) * width] + heard[b, q, j].astype(F32)
                        ).astype(BF16)
                    if q < NX - 1:
                        first[q].start()
        pump(b + 1, 8)
        kept = []
        for first, second, own, heard, out, seen, mine in (
            (a1, a2, sa, r1a, s1a, ys, y),
            (b1, b2, sb, r1b, s1b, xs, x),
        ):
            for copy in first:
                copy.wait_recv()

            def total_at(j):
                total = own[b, NX - 1, j].astype(F32)
                for q in range(NX - 1):
                    total = total + heard[b, q, j].astype(F32)
                return total

            for r in range(NX - 1):
                out[b, r] = total_at(seen[r]).astype(BF16)
                second[r].start()
            kept.append(total_at(mine))
        pump(b + 1, len(pieces[0]))
        if b + 2 < NZ:
            launch(b + 2)
        for rows, second, heard, total in ((rows_a, a2, r2a, kept[0]), (rows_b, b2, r2b, kept[1])):
            for r in range(NX - 1):
                second[r].wait_recv()
                total = total + heard[b, r].astype(F32)
            state[rows, :] = (state[rows, :] + total).astype(BF16).astype(F32)

    for b in range(LIVE):
        if b > 0:
            widen(b)
            unfold(b)
            conv(b)
        mix(b)
        if b == 0:
            @pl.when(last)
            def _():
                for copy in head_y:
                    copy.wait_recv()
                wait_bytes(w_last, local_sem.at[1])

                def fold(i, total):
                    whole = jnp.concatenate(
                        [heads[i, j, k] for j in range(NY) for k in range(NC)], axis=1
                    ).astype(BF16)
                    return total + nt(whole, w_last[:, pl.ds(pl.multiple_of(i * span, span), span)])

                w3h[...] = lax.fori_loop(0, NX, fold, jnp.zeros(w3h.shape, F32))
                for copy in w3h_out:
                    copy.start()

    widen(LIVE)
    unfold(LIVE)
    conv(LIVE)

    s_core = link(score_own.at[0], score_in.at[0], sibling)
    s_x = [link(score_own.at[1], score_in.at[1 + r], at_x[r]) for r in range(NX - 1)]
    s_y = [link(score_own.at[2], score_in.at[NX + r], at_y[r]) for r in range(NY - 1)]
    for r in range(NZ - 1):
        @pl.when(z == r)
        def _():
            w3h_out[r].wait_recv()

    scores = nt(head[...], state[...], HIGH) + nt(w3h[...], act[LIVE].astype(F32), HIGH)
    score_own[0] = scores
    s_core.start()
    s_core.wait_recv()
    scores = scores + score_in[0]
    score_own[1] = scores
    for copy in s_x:
        copy.start()
    for copy in s_x:
        copy.wait_recv()
    for r in range(NX - 1):
        scores = scores + score_in[1 + r]
    score_own[2] = scores
    for copy in s_y:
        copy.start()
    for copy in s_y:
        copy.wait_recv()
    for r in range(NY - 1):
        scores = scores + score_in[NX + r]
    classes = lax.broadcasted_iota(jnp.int32, scores.shape, 0)
    hot = (classes == labels[pl.ds(z, 1), :]).astype(F32)
    top = (jax.nn.sigmoid(scores) - hot) * (LOSS_SCALE / (NZ * steps))
    top_t = top.T
    back = nn(top_t, head[...], HIGH).astype(BF16).astype(F32)
    act_grad = nn(top_t, w3h[...], HIGH)

    def silu_grad(b, act_grad):
        value = conv_out[b]
        s = jax.nn.sigmoid(value)
        cgrad[b] = (act_grad * s * (1.0 + value * (1.0 - s))).astype(BF16)

    def input_grad(b):
        pad[pl.ds(edge, steps), :] = cgrad[b].astype(F32)
        total = jnp.zeros((steps, width), F32)
        for k in range(taps):
            shifted = pad[pl.ds(edge - k + half, steps), :].astype(BF16)
            total = total + nt(shifted, dense[b, pl.ds(k * width, width), :])
        return total

    kept_taps = [pl.ds(half + 1, taps - half - 1), pl.ds(0, half + 1)]
    starts = [1, 3]
    middles = [(2, 3), (2, 1)]

    def gc_copy(b, way):
        at = kept_taps[way]
        return remote(
            gcsend.at[b, at], gccrecv.at[b, at], gc_send.at[b, way], gc_recv.at[b, way], (up, down)[way]
        )

    def conv_weight_grad(b):
        whole = tn(cols[b], cgrad[b])
        for k in range(taps):
            piece = jnp.where(
                first_group,
                whole[k * width : k * width + group],
                whole[k * width + group : (k + 1) * width],
            )
            gcpart[b, k] = piece
            gcsend[b, k] = piece.astype(BF16)
        for way in range(2):
            @pl.when(is_z(b + starts[way]))
            def _():
                gc_copy(b, way).start()

    def conv_weight_relay(b):
        for way in range(2):
            @pl.when(is_z(*[b + m for m in middles[way]]))
            def _():
                gc_copy(b, way).wait_recv()
                at = kept_taps[way]
                gcsend[b, at] = (gcpart[b, at] + gccrecv[b, at].astype(F32)).astype(BF16)
                gc_copy(b, way).start()

    def gather_links(b):
        own_a, own_b = ga.at[b, NX - 1, NY - 1, c], gb.at[b, NY - 1, NX - 1, c]
        links = {
            "a1": [link(own_a, ga.at[b, NX - 1, r, c], at_y[r]) for r in range(NY - 1)],
            "b1": [link(own_b, gb.at[b, NY - 1, r, c], at_x[r]) for r in range(NX - 1)],
            "a2own": [link(own_a, ga.at[b, r, NY - 1, c], at_x[r]) for r in range(NX - 1)],
            "b2own": [link(own_b, gb.at[b, r, NX - 1, c], at_y[r]) for r in range(NY - 1)],
        }
        rest = pl.ds(0, NX - 1)
        line_a, line_b = ga.at[b, NX - 1, rest, c], gb.at[b, NY - 1, rest, c]
        links["a2"] = [link(line_a, ga.at[b, r, rest, c], at_x[r]) for r in range(NX - 1)]
        links["b2"] = [link(line_b, gb.at[b, r, rest, c], at_y[r]) for r in range(NY - 1)]
        links["ca"] = [link(ga.at[b, r, :, c], ga.at[b, r, :, c], sibling) for r in range(NX)]
        links["cb"] = [link(gb.at[b, r, :, c], gb.at[b, r, :, c], sibling) for r in range(NY)]
        return links

    def gather_start(b, links, back):
        ga[b, NX - 1, NY - 1, c] = back[:top_rows].astype(BF16)
        gb[b, NY - 1, NX - 1, c] = back[top_rows:].astype(BF16)
        for name in ("a1", "b1", "a2own", "b2own"):
            for copy in links[name]:
                copy.start()

    def gather_second(links):
        for p in "ab":
            for copy in links[p + "1"]:
                copy.wait_recv()
            for copy in links[p + "2"]:
                copy.start()
            links["c" + p][NX - 1].start()

    def gather_third(links):
        for r in range(NX - 1):
            for p in "ab":
                links[p + "2own"][r].wait_recv()
                links[p + "2"][r].wait_recv()
                links["c" + p][r].start()

    def pair_cols(px, py):
        return pl.ds(pl.multiple_of((px * NY + py) * pair, pair), pair)

    def act_grad_of(b, links):
        totals = [jnp.zeros((top_rows, width), F32) for _ in range(2)]
        for r in [NX - 1] + list(range(NX - 1)):
            for way, buffer in enumerate((ga, gb)):
                links[("ca", "cb")[way]][r].wait_recv()
                left = jnp.concatenate([buffer[b, r, s, k] for s in range(NY) for k in range(NC)], axis=1)
                right = jnp.concatenate(
                    [
                        w_all[b, :, pair_cols(xl[r], yl[s]) if way == 0 else pair_cols(xl[s], yl[r])]
                        for s in range(NY)
                    ],
                    axis=1,
                )
                totals[way] = totals[way] + nt(left, right)
        return jnp.concatenate(totals, axis=0)

    def gp_copy(b, r, s, device):
        return remote(gsend.at[b, r, s], crecv.at[b, r, s], gp_send.at[b, r, s], gp_recv.at[b, r, s], device)

    def point_grad(b):
        act_t = act[b].astype(F32).T.astype(BF16)
        turn = jnp.where(is_z(b + starts[0]), 2, 0)
        starter = is_z(b + starts[0], b + starts[1])
        device = {"section": jnp.where(is_z(b + starts[0]), zs[0], zs[2])}
        for slot in range(NX):
            r = lax.rem(slot + turn, NX)
            for s in range(NY):
                whole = jnp.concatenate(
                    [
                        jnp.concatenate([ga[b, r, s, k] for k in range(NC)], axis=1),
                        jnp.concatenate([gb[b, s, r, k] for k in range(NC)], axis=1),
                    ],
                    axis=0,
                )
                part = nn(act_t, whole)
                if slot < 2:
                    @pl.when(starter)
                    def _():
                        gsend[b, r, s] = part.astype(BF16)
                        gp_copy(b, r, s, device).start()

                    @pl.when(jnp.logical_not(starter))
                    def _():
                        gpart[r, s] = part
                else:
                    gpart[r, s] = part

        @pl.when(z == b)
        def _():
            ghome[...] = gpart[...]

    def point_relay(b, lo, hi):
        for j in range(lo, hi):
            for way in range(2):
                r, s = (2 if way == 0 else 0) + j // NY, j % NY

                @pl.when(is_z(*[b + m for m in middles[way]]))
                def _():
                    copy = gp_copy(b, r, s, (up, down)[way])
                    copy.wait_recv()
                    gsend[b, r, s] = (gpart[r, s] + crecv[b, r, s].astype(F32)).astype(BF16)
                    copy.start()

    silu_grad(LIVE, act_grad)
    back = (back + input_grad(LIVE)).astype(BF16).astype(F32)
    links = gather_links(LIVE - 1)
    gather_start(LIVE - 1, links, back)
    tsend[...] = nn(top, act[LIVE].astype(F32), HIGH)
    t_links = [
        link(tsend, trecv.at[d - 1], {"section": jnp.int32(NZ - 1)}, z == (NZ - 1 + d) % NZ) for d in range(1, NZ)
    ]
    for d in range(1, NZ):
        @pl.when(z == (NZ - 1 + d) % NZ)
        def _():
            t_links[d - 1].start()

    gather_second(links)
    conv_weight_grad(LIVE)
    for b in range(LIVE - 1, -1, -1):
        if b + 1 < LIVE:
            point_relay(b + 1, 0, 4)
        gather_third(links)
        conv_weight_relay(b + 1)
        if b + 1 < LIVE:
            point_relay(b + 1, 4, 8)
        silu_grad(b, act_grad_of(b, links))
        if b > 0:
            back = (back + input_grad(b)).astype(BF16).astype(F32)
            links = gather_links(b - 1)
            gather_start(b - 1, links, back)
        point_grad(b)
        if b > 0:
            gather_second(links)
        conv_weight_grad(b)
    point_relay(0, 0, 8)
    conv_weight_relay(0)

    def out_copy(r, s):
        return pltpu.make_async_copy(
            ghome.at[r, s], out_gp.at[0, :, pair_cols(xl[r], yl[s])], out_sem.at[r, s]
        )

    @pl.when(last)
    def _():
        total = tsend[...]
        for d in range(1, NZ):
            t_links[d - 1].wait_recv()
            total = total + trecv[d - 1]
        total_t = total.T
        for r in range(NX):
            for s in range(NY):
                whole = jnp.concatenate([heads[xl[r], yl[s], k] for k in range(NC)], axis=1)
                ghome[r, s] = nn(total_t, whole, HIGH)
                out_copy(r, s).start()

    for b in range(LIVE):
        @pl.when(z == b)
        def _():
            for j in range(2 * NY):
                for r, s in ((2 + j // NY, j % NY), (j // NY, j % NY)):
                    gp_copy(b, r, s, up).wait_recv()
                    ghome[r, s] = ghome[r, s] + crecv[b, r, s].astype(F32)
                    out_copy(r, s).start()

    for b in range(NZ):
        @pl.when(z == b)
        def _():
            for way in range(2):
                gc_copy(b, way).wait_recv()
            out_gc[0] = gcpart[b] + gccrecv[b].astype(F32)

    for r in range(NX):
        for s in range(NY):
            out_copy(r, s).wait()
    for copy, when in sent:
        if when is None:
            copy.wait_send()
        else:
            pl.when(when)(copy.wait_send)
    for b in range(NZ):
        @pl.when(z != b)
        def _():
            for way in range(2):
                gc_copy(b, way).wait_send()
            if b < LIVE:
                for r in range(NX):
                    for s in range(NY):
                        gp_copy(b, r, s, up).wait_send()
    assert count[0] <= send.shape[0], count[0]


def local(inputs, labels, conv_weight, point_weight, head_weight):
    steps, width = inputs.shape[1:]
    blocks, taps, group, _ = conv_weight.shape
    chans = point_weight.shape[2]
    part = steps // 2
    pair = NC * width
    head = jnp.pad(head_weight.astype(F32).T, ((0, 8 - CLASSES), (0, 0)))
    vmem = pl.BlockSpec(memory_space=pltpu.VMEM)
    hbm = pl.BlockSpec(memory_space=pl.ANY)
    V = pltpu.VMEM
    dma = pltpu.SemaphoreType.DMA
    scratch = [
        V((LIVE, width, chans), BF16),
        V((NZ, taps, group, width), BF16),
        V((width, chans), BF16),
        V((steps, width), BF16),
        V((NZ, taps * width, width), BF16),
        V((NZ, steps, taps * width), BF16),
        V((NZ, steps, width), F32),
        V((NZ, steps, width), BF16),
        V((steps, width), F32),
        V((steps + 16, width), F32),
        V((NZ, steps, width), BF16),
        V((LIVE, NX, NY, part, width), BF16),
        V((LIVE, NX, NY, part, width), BF16),
        V((LIVE, NY, NX, part, width), BF16),
        V((LIVE, NY, NX, part, width), BF16),
        V((LIVE, NX, NY, part, width), BF16),
        V((LIVE, NY, NX, part, width), BF16),
        V((LIVE, NX - 1, NY, part, width), BF16),
        V((LIVE, NY - 1, NX, part, width), BF16),
        V((LIVE, NY - 1, part, width), BF16),
        V((LIVE, NX - 1, part, width), BF16),
        V((LIVE, NY - 1, part, width), BF16),
        V((LIVE, NX - 1, part, width), BF16),
        V((LIVE, NX, NY, NC, part, width), BF16),
        V((LIVE, NY, NX, NC, part, width), BF16),
        V((LIVE, NX, NY, width, pair), BF16),
        V((LIVE, NX, NY, width, pair), BF16),
        V((NX, NY, width, pair), F32),
        V((NX, NY, width, pair), F32),
        V((NZ, taps, group, width), BF16),
        V((NZ, taps, group, width), BF16),
        V((NZ, taps, group, width), F32),
        V((NX, NY, NC, 8, width), F32),
        V((8, width), F32),
        V((8, width), F32),
        V((NZ - 1, 8, width), F32),
        V((3, 8, steps), F32),
        V((NX + NY - 1, 8, steps), F32),
        dma((320,)),
        dma((320,)),
        dma((LIVE, NX, NY)),
        dma((LIVE, NX, NY)),
        dma((NZ, 2)),
        dma((NZ, 2)),
        dma((2,)),
        dma((NX, NY)),
    ]
    return pl.pallas_call(
        kernel,
        out_shape=(
            jax.ShapeDtypeStruct(point_weight.shape, F32),
            jax.ShapeDtypeStruct(conv_weight.shape, F32),
        ),
        in_specs=[hbm, vmem, hbm, hbm, vmem],
        out_specs=(hbm, vmem),
        scratch_shapes=scratch,
        compiler_params=pltpu.CompilerParams(
            collective_id=0, has_side_effects=True, vmem_limit_bytes=58 * 1024 * 1024
        ),
    )(inputs, labels, conv_weight, point_weight, head)


def solution(mesh):
    placed = (
        P(None, None, "chan"),
        P(),
        P("section", None, None, "chan"),
        P("section", "chan", None),
        P("chan", None),
    )
    return jax.shard_map(
        local,
        mesh=mesh,
        in_specs=placed,
        out_specs=(P("section", "chan", None), P("section", None, None, "chan")),
        check_vma=False,
    )
```

time: 1230 us -> 192 us (0.16); the launches traced: 1210 us -> 190 us
  waiting for transfers between devices: 730 us -> 0 us
  Pallas kernels: 0 us -> 184 us
  local copies, waits for them, and re-layouts: 175 us -> 3.87 us
  matrix products: 124 us -> 0 us
  blocking collectives: 121 us -> 0 us
  starting transfers between devices: 28.8 us -> 0 us
  other arithmetic: 18.1 us -> 1.28 us
  between operations: 17.3 us -> 0.65 us
    unnamed x21 -> x0, waiting for transfers between devices: 554 us -> none
    pallas_call x0 -> x1, Pallas kernels: none -> 184 us  [local(): pl.pallas_call(kernel, out_shape=(jax.ShapeDtypeStruct(point_weight.shape...]
    all_gather x7 -> x0, waiting for transfers between devices: 152 us -> none  [local(): lax.all_gather(back, 'chan', axis=1, tiled=True)]
    psum x1 -> x0, blocking collectives: 121 us -> none  [local(): lax.psum(jnp.dot(state, head_weight, preferred_element_type=jnp.float32),...]
    dot_general x98 -> x0, matrix products: 87.4 us -> none  [the longest x63 41.1 us: kernel_grad(): jnp.einsum('tgi,tgo->igo', shifted, grads3, preferred_element_type=jnp.fl...]
    unnamed x234 -> x4, local copies, waits for them, and re-layouts: 71.9 us -> 3.87 us
    another operation x72 -> x0, local copies, waits for them, and re-layouts: 44.9 us -> none  [the longest x70 44.8 us: kernel_grad(): return jnp.stack(pieces)]
    conv_general_dilated x20 -> x0, matrix products: 37 us -> none  [conv_local(): lax.conv_general_dilated(field[None], kernel, (1,), [(half, half)], dimen...]
  transfers between devices with their start and end apart: 26 -> 0, of which waited for: 25 -> 0; matrix products, arithmetic and copies ran while one was open for 15% -> 0% of each run, Pallas kernels for 0% -> 0%
where the time goes in v2:
time: 192 us; the launch traced here: 190 us
  Pallas kernels  184 us (96%)
  local copies, waits for them, and re-layouts  3.87 us (2%)
    pallas_call x1, Pallas kernels, local(): pl.pallas_call(kernel, out_shape=(jax.ShapeDtypeStruct(point_weight.shape...  184 us
    unnamed x4, local copies, waits for them, and re-layouts  3.87 us

profile of v2, /device:TPU:1, one launch (start us, length us, event | category | flops | bytes accessed | tf_op | source)
XLA Modules:
  0.0 190.3 jit_solution(8777138045005409449)
XLA Ops:
  0.6 1.3 pad_convert_fusion.head
  1.9 184.5 %shard_map.68 = (f32[1,128,4096]{2,1,0:T(8,128)}, f32[1,9,64,128]{3,2,1,0:T(8,128)}) custom-call(bf16[4,256,128]{2,1,0:T(8,128)(2,1)} %inputs.1, s32[4,256]{1,0:T(4,128)} %labels.1, bf16[1,9,64,128]{3,2,1,0:T(8,128)(2,1)} %cw.1, bf16[1,128,4096]{2,1,0:T(8,128)(2,1)} %pw.1, f32[8,128]{1,0:T(8,128)} %pad_convert_fusion.head), custom_call_target="tpu_custom_call" | custom-call | tf_op jit(solution)/shard_map/pallas_call | solution.py:651
  186.4 0.0 copy-start
  186.4 3.2 %copy.9 = f32[1,128,4096]{2,1,0:T(8,128)} copy(f32[1,128,4096]{2,1,0:T(8,128)} %get-tuple-element.4) | data formatting | bytes 4194304
  189.6 0.0 copy-done
  189.6 0.7 copy.10
Async XLA Ops:
  186.4 3.2 %copy-start = (f32[1,9,64,128]{3,2,1,0:T(8,128)S(1)}, f32[1,9,64,128]{3,2,1,0:T(8,128)}, u32[]{:S(2)}) copy-start(f32[1,9,64,128]{3,2,1,0:T(8,128)} %get-tuple-element.5) | copy-start | bytes 884740

commit v3 on v2

--- a/solution.py
+++ b/solution.py
@@ -1,3 +1,5 @@
+import functools
+
 import jax
 import jax.numpy as jnp
 from jax import lax
@@ -32,13 +34,13 @@
 
 
 def kernel(
-    inputs, labels, cw, pw, head,
+    inputs, labels_in, cw, pw, head_in,
     out_gp, out_gc,
-    w_all, cw_all, w_last, start, dense, cols, conv_out, act, state, pad, cgrad,
+    labels, head_raw, head, w_all, cw_all, w_last, start, dense, cols, conv_out, act, state, pad, cgrad,
     pas, par, pbs, pbr, sa, sb, r1a, r1b, s1a, s1b, r2a, r2b,
-    ga, gb, gsend, crecv, gpart, ghome, gcsend, gccrecv, gcpart,
+    ga, gb, gsend, crecv, hrecv, gpart, ghome, gcsend, gccrecv, gcpart,
     heads, w3h, tsend, trecv, score_own, score_in,
-    send, recv, gp_send, gp_recv, gc_send, gc_recv, local_sem, out_sem,
+    send, recv, gp_send, gp_recv, home_gp, local_sem, out_sem,
 ):
     steps, width = start.shape
     taps, group = cw.shape[1], cw.shape[2]
@@ -71,7 +73,6 @@
         return hit
 
     count = [0]
-    sent = []
 
     def number():
         count[0] += 1
@@ -83,13 +84,25 @@
             device_id=device, device_id_type=MESH,
         )
 
+    sends = [0]
+    drains = []
+
+    def lane_of(total, when=None):
+        sends[0] += 1
+        sem = send.at[sends[0] - 1]
+        drains.append((total, sem, when))
+        return sem
+
+    def fan(copies, total, when=None):
+        sem = lane_of(total, when)
+        return [remote(src, dst, sem, recv.at[number()], device) for src, dst, device in copies]
+
     def link(src, dst, device, when=None):
-        n = number()
-        copy = remote(src, dst, send.at[n], recv.at[n], device)
-        sent.append((copy, when))
-        return copy
+        return fan([(src, dst, device)], src, when)[0]
 
     pltpu.make_async_copy(inputs.at[z], start, local_sem.at[0]).start()
+    pltpu.make_async_copy(labels_in, labels, local_sem.at[2]).start()
+    pltpu.make_async_copy(head_in, head_raw, local_sem.at[3]).start()
 
     @pl.when(last)
     def _():
@@ -102,71 +115,82 @@
     pl.semaphore_wait(barrier, len(peers))
 
     class Piece:
-        def __init__(self, b, way, src, ref):
-            n = number()
-            self.src, self.ref, self.sem, self.b = src, ref, recv.at[n], b
+        def __init__(self, b, way, src, ref, sem):
+            self.src, self.ref, self.sem = src, ref, recv.at[number()]
             device = (up, down)[way]
-            order = [b + 1, b + 2, b + 3] if way == 0 else [b + 3, b + 2, b + 1]
-            self.relays = is_z(*order[:2])
-            self.first = remote(src, ref, send.at[n], recv.at[n], device)
-            self.next = remote(ref, ref, send.at[n], recv.at[n], device)
-            sent.append((self.next, z != order[2] % NZ))
-
-        def relay(self):
-            @pl.when(self.relays)
+            self.order = [b + 1, b + 2, b + 3] if way == 0 else [b + 3, b + 2, b + 1]
+            self.first = remote(src, ref, sem, self.sem, device)
+            self.next = remote(ref, ref, sem, self.sem, device)
+
+        def relay(self, hop):
+            @pl.when(is_z(self.order[hop]))
             def _():
                 wait_bytes(self.ref, self.sem)
                 self.next.start()
 
         def ready(self):
-            @pl.when(jnp.logical_not(self.relays))
+            @pl.when(jnp.logical_not(is_z(*self.order[:2])))
             def _():
                 wait_bytes(self.ref, self.sem)
 
-    def broadcast(b):
-        ways = []
+    taps_of, columns_of = [], []
+    for b in range(NZ):
         for way in range(2):
+            end = z != (b + (3, 1)[way]) % NZ
             kept = pl.ds(0, half + 1) if way == 0 else pl.ds(half + 1, taps - half - 1)
-            pieces = [Piece(b, way, cw.at[0, kept], cw_all.at[b, kept])]
+            ref = cw_all.at[b, kept]
+            taps_of.append(Piece(b, way, cw.at[0, kept], ref, lane_of(ref, end)))
             if b < LIVE:
+                sem = lane_of(w_all.at[b, :, pl.ds(0, 2 * span)], end)
+                pieces = []
                 for r in range(way, NX, 2):
                     for k in range(SUB):
                         size = span // SUB
                         at = pl.ds(pl.multiple_of(xs[r] * span + k * size, size), size)
-                        pieces.append(Piece(b, way, pw.at[0, :, at], w_all.at[b, :, at]))
-            ways.append(pieces)
-        return [piece for both in zip(*ways) for piece in both]
-
-    pieces = [broadcast(b) for b in range(NZ)]
-
-    def launch(b):
+                        pieces.append(Piece(b, way, pw.at[0, :, at], w_all.at[b, :, at], sem))
+                columns_of.append(pieces)
+
+    def launch(b, pieces):
         @pl.when(z == b)
         def _():
-            for piece in pieces[b]:
+            for piece in pieces:
                 piece.first.start()
-            for piece in pieces[b]:
+            for piece in pieces:
                 pltpu.make_async_copy(piece.src, piece.ref, piece.sem).start()
 
-    pumped = [0] * NZ
-
-    def pump(b, amount):
-        for piece in pieces[b][pumped[b] : pumped[b] + amount]:
-            piece.relay()
-        pumped[b] += amount
+    def both(b):
+        return [piece for two in zip(columns_of[2 * b], columns_of[2 * b + 1]) for piece in two]
+
+    def relays(pieces, hop, lo=0, hi=None):
+        for piece in pieces[lo:hi]:
+            piece.relay(hop)
 
     head_core = link(heads.at[x, y, c], heads.at[x, y, c], sibling, last)
     head_x = [link(heads.at[x, y], heads.at[x, y], at_x[r], last) for r in range(NX - 1)]
     head_y = [link(heads.at[:, y], heads.at[:, y], at_y[r], last) for r in range(NY - 1)]
     w3h_out = [link(w3h, w3h, {"section": zs[r]}, last) for r in range(NZ - 1)]
 
-    launch(0)
+    launch(0, taps_of[:2] + both(0))
+    for b in range(1, NZ):
+        launch(b, taps_of[2 * b : 2 * b + 2])
+    launch(1, columns_of[3])
+
+    wait_bytes(labels_in, local_sem.at[2])
+    wait_bytes(head_in, local_sem.at[3])
+    picked = (
+        lax.broadcasted_iota(jnp.int32, (head.shape[0], CLASSES), 0)
+        == lax.broadcasted_iota(jnp.int32, (head.shape[0], CLASSES), 1)
+    ).astype(F32)
+    head[...] = nt(picked, head_raw[...].astype(F32))
 
     @pl.when(last)
     def _():
         heads[x, y, c] = head[...]
         head_core.start()
 
-    pump(0, 2)
+    for piece in taps_of[:2] + both(0)[: 2 * SUB]:
+        piece.relay(0)
+        piece.relay(1)
 
     @pl.when(last)
     def _():
@@ -188,7 +212,7 @@
             cols[b, :, pl.ds(k * width, width)] = pad[pl.ds(edge + k - half, steps), :].astype(BF16)
 
     def widen(b):
-        for piece in pieces[b][:2]:
+        for piece in taps_of[2 * b : 2 * b + 2]:
             piece.ready()
         for k in range(taps):
             tap = cw_all[b, k].astype(F32)
@@ -201,7 +225,9 @@
         act[b] = (value * jax.nn.sigmoid(value)).astype(BF16)
 
     unfold(0)
-    pump(0, len(pieces[0]) // 2)
+    for piece in both(0)[2 * SUB : 3 * SUB]:
+        piece.relay(0)
+        piece.relay(1)
 
     @pl.when(last)
     def _():
@@ -212,16 +238,20 @@
 
     widen(0)
     conv(0)
-    pump(0, len(pieces[0]))
-    launch(1)
+    for piece in both(0)[3 * SUB :]:
+        piece.relay(0)
+        piece.relay(1)
+    relays(taps_of[2:], 0)
+    launch(1, columns_of[2])
+    launch(2, columns_of[5])
 
     def mix(b):
-        ca = [link(pas.at[b, r], par.at[b, r], sibling) for r in range(NX)]
-        cb = [link(pbs.at[b, r], pbr.at[b, r], sibling) for r in range(NY)]
-        a1 = [link(sa.at[b, r], r1a.at[b, r], at_x[r]) for r in range(NX - 1)]
-        b1 = [link(sb.at[b, r], r1b.at[b, r], at_y[r]) for r in range(NY - 1)]
-        a2 = [link(s1a.at[b, r], r2a.at[b, r], at_y[r]) for r in range(NY - 1)]
-        b2 = [link(s1b.at[b, r], r2b.at[b, r], at_x[r]) for r in range(NX - 1)]
+        ca = fan([(pas.at[b, r], par.at[b, r], sibling) for r in range(NX)], pas.at[b])
+        cb = fan([(pbs.at[b, r], pbr.at[b, r], sibling) for r in range(NY)], pbs.at[b])
+        a1 = fan([(sa.at[b, r], r1a.at[b, r], at_x[r]) for r in range(NX - 1)], r1a.at[b])
+        b1 = fan([(sb.at[b, r], r1b.at[b, r], at_y[r]) for r in range(NY - 1)], r1b.at[b])
+        a2 = fan([(s1a.at[b, r], r2a.at[b, r], at_y[r]) for r in range(NY - 1)], r2a.at[b])
+        b2 = fan([(s1b.at[b, r], r2b.at[b, r], at_x[r]) for r in range(NX - 1)], r2b.at[b])
 
         def weights(place, core):
             return jnp.concatenate(
@@ -238,7 +268,7 @@
         def line_b(r):
             return lambda i: i * NY + ys[r]
 
-        for piece in pieces[b][2:]:
+        for piece in both(b):
             piece.ready()
         for r in range(NX + 1):
             if r < NX:
@@ -261,7 +291,13 @@
                         ).astype(BF16)
                     if q < NX - 1:
                         first[q].start()
-        pump(b + 1, 8)
+        if b == 0:
+            relays(taps_of[2:], 1)
+            relays(columns_of[2], 0, 0, 5)
+            relays(columns_of[3], 1, 0, 5)
+        if b == 1:
+            relays(columns_of[5], 1, 0, 4)
+            relays(columns_of[4], 0, 0, 5)
         kept = []
         for first, second, own, heard, out, seen, mine in (
             (a1, a2, sa, r1a, s1a, ys, y),
@@ -269,6 +305,12 @@
         ):
             for copy in first:
                 copy.wait_recv()
+            if first is b1:
+                if b == 0:
+                    relays(columns_of[2], 0, 5)
+                    relays(columns_of[3], 1, 5)
+                if b == 1:
+                    relays(columns_of[4], 0, 5)
 
             def total_at(j):
                 total = own[b, NX - 1, j].astype(F32)
@@ -280,9 +322,15 @@
                 out[b, r] = total_at(seen[r]).astype(BF16)
                 second[r].start()
             kept.append(total_at(mine))
-        pump(b + 1, len(pieces[0]))
-        if b + 2 < NZ:
-            launch(b + 2)
+        if b == 0:
+            launch(2, columns_of[4])
+            relays(columns_of[3], 0)
+            relays(columns_of[5], 0)
+            relays(columns_of[2], 1)
+        if b == 1:
+            relays(columns_of[5], 1, 4)
+            relays(columns_of[4], 1)
+        widen(b + 1)
         for rows, second, heard, total in ((rows_a, a2, r2a, kept[0]), (rows_b, b2, r2b, kept[1])):
             for r in range(NX - 1):
                 second[r].wait_recv()
@@ -291,7 +339,6 @@
 
     for b in range(LIVE):
         if b > 0:
-            widen(b)
             unfold(b)
             conv(b)
         mix(b)
@@ -312,7 +359,6 @@
                 for copy in w3h_out:
                     copy.start()
 
-    widen(LIVE)
     unfold(LIVE)
     conv(LIVE)
 
@@ -363,54 +409,54 @@
             total = total + nt(shifted, dense[b, pl.ds(k * width, width), :])
         return total
 
-    kept_taps = [pl.ds(half + 1, taps - half - 1), pl.ds(0, half + 1)]
     starts = [1, 3]
     middles = [(2, 3), (2, 1)]
-
-    def gc_copy(b, way):
-        at = kept_taps[way]
-        return remote(
-            gcsend.at[b, at], gccrecv.at[b, at], gc_send.at[b, way], gc_recv.at[b, way], (up, down)[way]
-        )
+    home_sems = [recv.at[number()] for _ in range(NZ - 1)]
 
     def conv_weight_grad(b):
         whole = tn(cols[b], cgrad[b])
-        for k in range(taps):
-            piece = jnp.where(
+        sem = lane_of(gcsend.at[b], z != b)
+
+        def piece(k):
+            return jnp.where(
                 first_group,
                 whole[k * width : k * width + group],
                 whole[k * width + group : (k + 1) * width],
             )
-            gcpart[b, k] = piece
-            gcsend[b, k] = piece.astype(BF16)
-        for way in range(2):
-            @pl.when(is_z(b + starts[way]))
+
+        @pl.when(z == b)
+        def _():
+            for k in range(taps):
+                gcpart[k] = piece(k)
+
+        @pl.when(z != b)
+        def _():
+            for k in range(taps):
+                gcsend[b, k] = piece(k).astype(BF16)
+
+        for d in range(1, NZ):
+            @pl.when(is_z(b + d))
             def _():
-                gc_copy(b, way).start()
-
-    def conv_weight_relay(b):
-        for way in range(2):
-            @pl.when(is_z(*[b + m for m in middles[way]]))
-            def _():
-                gc_copy(b, way).wait_recv()
-                at = kept_taps[way]
-                gcsend[b, at] = (gcpart[b, at] + gccrecv[b, at].astype(F32)).astype(BF16)
-                gc_copy(b, way).start()
+                remote(
+                    gcsend.at[b], gccrecv.at[d - 1], sem, home_sems[d - 1], {"section": jnp.int32(b)}
+                ).start()
 
     def gather_links(b):
         own_a, own_b = ga.at[b, NX - 1, NY - 1, c], gb.at[b, NY - 1, NX - 1, c]
+        three = r2a.at[0]
+        rest = pl.ds(0, NX - 1)
+        nine = r1a.at[0, rest, rest]
+        line_a, line_b = ga.at[b, NX - 1, rest, c], gb.at[b, NY - 1, rest, c]
         links = {
-            "a1": [link(own_a, ga.at[b, NX - 1, r, c], at_y[r]) for r in range(NY - 1)],
-            "b1": [link(own_b, gb.at[b, NY - 1, r, c], at_x[r]) for r in range(NX - 1)],
-            "a2own": [link(own_a, ga.at[b, r, NY - 1, c], at_x[r]) for r in range(NX - 1)],
-            "b2own": [link(own_b, gb.at[b, r, NX - 1, c], at_y[r]) for r in range(NY - 1)],
+            "a1": fan([(own_a, ga.at[b, NX - 1, r, c], at_y[r]) for r in range(NY - 1)], three),
+            "b1": fan([(own_b, gb.at[b, NY - 1, r, c], at_x[r]) for r in range(NX - 1)], three),
+            "a2own": fan([(own_a, ga.at[b, r, NY - 1, c], at_x[r]) for r in range(NX - 1)], three),
+            "b2own": fan([(own_b, gb.at[b, r, NX - 1, c], at_y[r]) for r in range(NY - 1)], three),
+            "a2": fan([(line_a, ga.at[b, r, rest, c], at_x[r]) for r in range(NX - 1)], nine),
+            "b2": fan([(line_b, gb.at[b, r, rest, c], at_y[r]) for r in range(NY - 1)], nine),
+            "ca": fan([(ga.at[b, r, :, c], ga.at[b, r, :, c], sibling) for r in range(NX)], pas.at[0]),
+            "cb": fan([(gb.at[b, r, :, c], gb.at[b, r, :, c], sibling) for r in range(NY)], pbs.at[0]),
         }
-        rest = pl.ds(0, NX - 1)
-        line_a, line_b = ga.at[b, NX - 1, rest, c], gb.at[b, NY - 1, rest, c]
-        links["a2"] = [link(line_a, ga.at[b, r, rest, c], at_x[r]) for r in range(NX - 1)]
-        links["b2"] = [link(line_b, gb.at[b, r, rest, c], at_y[r]) for r in range(NY - 1)]
-        links["ca"] = [link(ga.at[b, r, :, c], ga.at[b, r, :, c], sibling) for r in range(NX)]
-        links["cb"] = [link(gb.at[b, r, :, c], gb.at[b, r, :, c], sibling) for r in range(NY)]
         return links
 
     def gather_start(b, links, back):
@@ -454,8 +500,13 @@
                 totals[way] = totals[way] + nt(left, right)
         return jnp.concatenate(totals, axis=0)
 
+    def home_copy(b, side, r, s):
+        return remote(
+            gsend.at[b, r, s], hrecv.at[side, r, s], gp_send.at[b], home_gp.at[side, r, s], (down, up)[side]
+        )
+
     def gp_copy(b, r, s, device):
-        return remote(gsend.at[b, r, s], crecv.at[b, r, s], gp_send.at[b, r, s], gp_recv.at[b, r, s], device)
+        return remote(gsend.at[b, r, s], crecv.at[b, r, s], gp_send.at[b], gp_recv.at[b, r, s], device)
 
     def point_grad(b):
         act_t = act[b].astype(F32).T.astype(BF16)
@@ -473,7 +524,7 @@
                     axis=0,
                 )
                 part = nn(act_t, whole)
-                if slot < 2:
+                if slot < 2 and b == 0:
                     @pl.when(starter)
                     def _():
                         gsend[b, r, s] = part.astype(BF16)
@@ -481,24 +532,57 @@
 
                     @pl.when(jnp.logical_not(starter))
                     def _():
-                        gpart[r, s] = part
+                        gpart[b % 2, r, s] = part
+                elif b > 0:
+                    far = is_z(b + 2)
+
+                    @pl.when(far)
+                    def _():
+                        gsend[b, r, s] = part.astype(BF16)
+                        gp_copy(b, r, s, (down, up)[slot // 2]).start()
+
+                    if slot < 2:
+                        for side in range(2):
+                            @pl.when(is_z(b + starts[side]))
+                            def _():
+                                gsend[b, r, s] = part.astype(BF16)
+                                home_copy(b, side, r, s).start()
+
+                        @pl.when(z == b)
+                        def _():
+                            gpart[b % 2, r, s] = part
+                    else:
+                        @pl.when(jnp.logical_not(far))
+                        def _():
+                            gpart[b % 2, r, s] = part
                 else:
-                    gpart[r, s] = part
+                    gpart[b % 2, r, s] = part
 
         @pl.when(z == b)
         def _():
-            ghome[...] = gpart[...]
-
-    def point_relay(b, lo, hi):
+            ghome[...] = gpart[b % 2]
+
+    def side_relay(b, lo, hi):
+        for j in range(lo, hi):
+            for side in range(2):
+                r, s = 2 * side + j // NY, j % NY
+
+                @pl.when(is_z(b + starts[side]))
+                def _():
+                    gp_copy(b, r, s, up).wait_recv()
+                    gsend[b, r, s] = (gpart[b % 2, r, s] + crecv[b, r, s].astype(F32)).astype(BF16)
+                    home_copy(b, side, r, s).start()
+
+    def point_relay(b, hop, lo, hi):
         for j in range(lo, hi):
             for way in range(2):
                 r, s = (2 if way == 0 else 0) + j // NY, j % NY
 
-                @pl.when(is_z(*[b + m for m in middles[way]]))
+                @pl.when(is_z(b + middles[way][hop]))
                 def _():
                     copy = gp_copy(b, r, s, (up, down)[way])
                     copy.wait_recv()
-                    gsend[b, r, s] = (gpart[r, s] + crecv[b, r, s].astype(F32)).astype(BF16)
+                    gsend[b, r, s] = (gpart[b % 2, r, s] + crecv[b, r, s].astype(F32)).astype(BF16)
                     copy.start()
 
     silu_grad(LIVE, act_grad)
@@ -506,8 +590,10 @@
     links = gather_links(LIVE - 1)
     gather_start(LIVE - 1, links, back)
     tsend[...] = nn(top, act[LIVE].astype(F32), HIGH)
+    t_sem = lane_of(tsend, z != NZ - 1)
     t_links = [
-        link(tsend, trecv.at[d - 1], {"section": jnp.int32(NZ - 1)}, z == (NZ - 1 + d) % NZ) for d in range(1, NZ)
+        remote(tsend, trecv.at[d - 1], t_sem, recv.at[number()], {"section": jnp.int32(NZ - 1)})
+        for d in range(1, NZ)
     ]
     for d in range(1, NZ):
         @pl.when(z == (NZ - 1 + d) % NZ)
@@ -517,12 +603,9 @@
     gather_second(links)
     conv_weight_grad(LIVE)
     for b in range(LIVE - 1, -1, -1):
-        if b + 1 < LIVE:
-            point_relay(b + 1, 0, 4)
+        if b + 2 < LIVE:
+            side_relay(b + 2, 0, 8)
         gather_third(links)
-        conv_weight_relay(b + 1)
-        if b + 1 < LIVE:
-            point_relay(b + 1, 4, 8)
         silu_grad(b, act_grad_of(b, links))
         if b > 0:
             back = (back + input_grad(b)).astype(BF16).astype(F32)
@@ -532,12 +615,16 @@
         if b > 0:
             gather_second(links)
         conv_weight_grad(b)
-    point_relay(0, 0, 8)
-    conv_weight_relay(0)
+    side_relay(1, 0, 8)
+    for j in range(0, 8, 2):
+        point_relay(0, 0, j, j + 2)
+        if j:
+            point_relay(0, 1, j - 2, j)
+    point_relay(0, 1, 6, 8)
 
     def out_copy(r, s):
         return pltpu.make_async_copy(
-            ghome.at[r, s], out_gp.at[0, :, pair_cols(xl[r], yl[s])], out_sem.at[r, s]
+            ghome.at[r, s], out_gp.at[0, :, pair_cols(xl[r], yl[s])], out_sem.at[0]
         )
 
     @pl.when(last)
@@ -558,35 +645,34 @@
         def _():
             for j in range(2 * NY):
                 for r, s in ((2 + j // NY, j % NY), (j // NY, j % NY)):
-                    gp_copy(b, r, s, up).wait_recv()
-                    ghome[r, s] = ghome[r, s] + crecv[b, r, s].astype(F32)
+                    if b == 0:
+                        gp_copy(b, r, s, up).wait_recv()
+                        heard = crecv[b, r, s].astype(F32)
+                    else:
+                        for side in range(2):
+                            home_copy(b, side, r, s).wait_recv()
+                        heard = hrecv[0, r, s].astype(F32) + hrecv[1, r, s].astype(F32)
+                    ghome[r, s] = ghome[r, s] + heard
                     out_copy(r, s).start()
 
-    for b in range(NZ):
-        @pl.when(z == b)
-        def _():
-            for way in range(2):
-                gc_copy(b, way).wait_recv()
-            out_gc[0] = gcpart[b] + gccrecv[b].astype(F32)
-
-    for r in range(NX):
-        for s in range(NY):
-            out_copy(r, s).wait()
-    for copy, when in sent:
+    total = gcpart[...]
+    for d in range(1, NZ):
+        wait_bytes(gccrecv.at[d - 1], home_sems[d - 1])
+        total = total + gccrecv[d - 1].astype(F32)
+    gcpart[...] = total
+    gc_out = pltpu.make_async_copy(gcpart, out_gc.at[0], out_sem.at[1])
+    gc_out.start()
+    for b in range(LIVE):
+        drains.append((gsend.at[b], gp_send.at[b], z != b))
+    for ref, sem, when in drains:
         if when is None:
-            copy.wait_send()
+            wait_bytes(ref, sem)
         else:
-            pl.when(when)(copy.wait_send)
-    for b in range(NZ):
-        @pl.when(z != b)
-        def _():
-            for way in range(2):
-                gc_copy(b, way).wait_send()
-            if b < LIVE:
-                for r in range(NX):
-                    for s in range(NY):
-                        gp_copy(b, r, s, up).wait_send()
-    assert count[0] <= send.shape[0], count[0]
+            pl.when(when)(functools.partial(wait_bytes, ref, sem))
+    wait_bytes(ghome, out_sem.at[0])
+    gc_out.wait()
+    assert sends[0] <= send.shape[0], sends[0]
+    assert count[0] <= recv.shape[0], count[0]
 
 
 def local(inputs, labels, conv_weight, point_weight, head_weight):
@@ -595,12 +681,13 @@
     chans = point_weight.shape[2]
     part = steps // 2
     pair = NC * width
-    head = jnp.pad(head_weight.astype(F32).T, ((0, 8 - CLASSES), (0, 0)))
-    vmem = pl.BlockSpec(memory_space=pltpu.VMEM)
     hbm = pl.BlockSpec(memory_space=pl.ANY)
     V = pltpu.VMEM
     dma = pltpu.SemaphoreType.DMA
     scratch = [
+        V(labels.shape, labels.dtype),
+        V(head_weight.shape, BF16),
+        V((8, width), F32),
         V((LIVE, width, chans), BF16),
         V((NZ, taps, group, width), BF16),
         V((width, chans), BF16),
@@ -628,25 +715,25 @@
         V((LIVE, NY, NX, NC, part, width), BF16),
         V((LIVE, NX, NY, width, pair), BF16),
         V((LIVE, NX, NY, width, pair), BF16),
-        V((NX, NY, width, pair), F32),
+        V((2, NX, NY, width, pair), BF16),
+        V((2, NX, NY, width, pair), F32),
         V((NX, NY, width, pair), F32),
         V((NZ, taps, group, width), BF16),
-        V((NZ, taps, group, width), BF16),
-        V((NZ, taps, group, width), F32),
+        V((NZ - 1, taps, group, width), BF16),
+        V((taps, group, width), F32),
         V((NX, NY, NC, 8, width), F32),
         V((8, width), F32),
         V((8, width), F32),
         V((NZ - 1, 8, width), F32),
         V((3, 8, steps), F32),
         V((NX + NY - 1, 8, steps), F32),
-        dma((320,)),
-        dma((320,)),
+        dma((80,)),
+        dma((222,)),
+        dma((LIVE,)),
         dma((LIVE, NX, NY)),
-        dma((LIVE, NX, NY)),
-        dma((NZ, 2)),
-        dma((NZ, 2)),
+        dma((2, NX, NY)),
+        dma((4,)),
         dma((2,)),
-        dma((NX, NY)),
     ]
     return pl.pallas_call(
         kernel,
@@ -654,13 +741,13 @@
             jax.ShapeDtypeStruct(point_weight.shape, F32),
             jax.ShapeDtypeStruct(conv_weight.shape, F32),
         ),
-        in_specs=[hbm, vmem, hbm, hbm, vmem],
-        out_specs=(hbm, vmem),
+        in_specs=[hbm] * 5,
+        out_specs=(hbm, hbm),
         scratch_shapes=scratch,
         compiler_params=pltpu.CompilerParams(
             collective_id=0, has_side_effects=True, vmem_limit_bytes=58 * 1024 * 1024
         ),
-    )(inputs, labels, conv_weight, point_weight, head)
+    )(inputs, labels, conv_weight, point_weight, head_weight)
 
 
 def solution(mesh):

time: 192 us -> 181 us (0.943)
  Pallas kernels: 184 us -> 175 us
    pallas_call x1, Pallas kernels: 184 us -> 175 us  [local(): pl.pallas_call(kernel, out_shape=(jax.ShapeDtypeStruct(point_weight.shape...]
    unnamed x4 -> x5, local copies, waits for them, and re-layouts: 3.87 us -> 5.28 us
where the time goes in v3:
time: 181 us
  Pallas kernels  175 us (97%)
  local copies, waits for them, and re-layouts  5.28 us (3%)
    pallas_call x1, Pallas kernels, local(): pl.pallas_call(kernel, out_shape=(jax.ShapeDtypeStruct(point_weight.shape...  175 us
    unnamed x5, local copies, waits for them, and re-layouts  5.28 us

profile of v3, /device:TPU:1, one launch (start us, length us, event | category | flops | bytes accessed | tf_op | source)
XLA Modules:
  0.0 180.8 jit_solution(2843845711745213062)
XLA Ops:
  0.6 1.4 copy.7.head_in
  2.0 174.8 %shard_map.68 = (f32[1,128,4096]{2,1,0:T(8,128)}, f32[1,9,64,128]{3,2,1,0:T(8,128)}) custom-call(bf16[4,256,128]{2,1,0:T(8,128)(2,1)} %inputs.1, s32[4,256]{1,0:T(4,128)} %labels_in.1, bf16[1,9,64,128]{3,2,1,0:T(8,128)(2,1)} %cw.1, bf16[1,128,4096]{2,1,0:T(8,128)(2,1)} %pw.1, bf16[128,3]{1,0:T(8,128)(2,1)} %copy.7.head_in), custom_call_target="tpu_custom_call" | custom-call | tf_op jit(solution)/shard_map/pallas_call | solution.py:738
  176.9 0.0 copy-start
  176.9 3.2 %copy.10 = f32[1,128,4096]{2,1,0:T(8,128)} copy(f32[1,128,4096]{2,1,0:T(8,128)} %get-tuple-element.4) | data formatting | bytes 4194304
  180.0 0.0 copy-done
  180.0 0.7 copy.11
Async XLA Ops:
  176.9 3.2 %copy-start = (f32[1,9,64,128]{3,2,1,0:T(8,128)S(1)}, f32[1,9,64,128]{3,2,1,0:T(8,128)}, u32[]{:S(2)}) copy-start(f32[1,9,64,128]{3,2,1,0:T(8,128)} %get-tuple-element.5) | copy-start | bytes 884740

commit v4 on v3

--- a/solution.py
+++ b/solution.py
@@ -225,6 +225,7 @@
         act[b] = (value * jax.nn.sigmoid(value)).astype(BF16)
 
     unfold(0)
+    relays(taps_of[2:], 0)
     for piece in both(0)[2 * SUB : 3 * SUB]:
         piece.relay(0)
         piece.relay(1)
@@ -241,9 +242,43 @@
     for piece in both(0)[3 * SUB :]:
         piece.relay(0)
         piece.relay(1)
-    relays(taps_of[2:], 0)
+    relays(taps_of[2:], 1)
+
+    @pl.when(z == 0)
+    def _():
+        for piece in columns_of[3]:
+            wait_bytes(piece.ref, piece.sem)
+        for piece in columns_of[3]:
+            piece.next.start()
+
     launch(1, columns_of[2])
     launch(2, columns_of[5])
+
+    up1, down1, up2, down2 = columns_of[2:6]
+    plan = {
+        (0, "early"): [(down1, 1, 0, 4), (up1, 0, 0, 1)],
+        (0, 1): [(down1, 1, 4, 5), (up1, 0, 1, 2)],
+        (0, 2): [(down1, 1, 5, 6), (up1, 0, 2, 3)],
+        (0, 3): [(up1, 0, 3, 4)],
+        (0, 4): [(down1, 1, 6, 7)],
+        (0, "sent"): [(down1, 1, 7, 8), (up1, 0, 4, 6), (up1, 1, 0, 2), (down2, 0, 0, 2)],
+        (0, "middle"): [(up1, 0, 6, 8), (up1, 1, 2, 5), (down2, 0, 2, 5)],
+        (0, "late"): [(up1, 1, 5, 8), (down2, 0, 5, 8)],
+        (1, "early"): [(down2, 1, 0, 5)],
+        (1, 1): [(down2, 1, 5, 6), (up2, 0, 0, 1)],
+        (1, 2): [(down2, 1, 6, 7), (up2, 0, 1, 2)],
+        (1, 3): [(down2, 1, 7, 8), (up2, 0, 2, 3)],
+        (1, "sent"): [(up2, 0, 3, 4), (up2, 1, 0, 1)],
+        (1, "middle"): [(up2, 0, 4, 7), (up2, 1, 1, 4)],
+        (1, "late"): [(up2, 0, 7, 8), (up2, 1, 4, 7)],
+        (1, "after"): [(up2, 1, 7, 8)],
+    }
+
+    def slot(b, name):
+        for pieces, hop, lo, hi in plan.get((b, name), []):
+            relays(pieces, hop, lo, hi)
+        if (b, name) == (0, "middle"):
+            launch(2, up2)
 
     def mix(b):
         ca = fan([(pas.at[b, r], par.at[b, r], sibling) for r in range(NX)], pas.at[b])
@@ -268,6 +303,7 @@
         def line_b(r):
             return lambda i: i * NY + ys[r]
 
+        slot(b, "early")
         for piece in both(b):
             piece.ready()
         for r in range(NX + 1):
@@ -277,6 +313,7 @@
                     for j in range(NY):
                         out[b, r, j] = part[:, j * width : (j + 1) * width].astype(BF16)
                     copy[r].start()
+            slot(b, r)
             if r >= 1:
                 q = r - 1
                 for rows, line, heard, out, copy, first in (
@@ -291,13 +328,7 @@
                         ).astype(BF16)
                     if q < NX - 1:
                         first[q].start()
-        if b == 0:
-            relays(taps_of[2:], 1)
-            relays(columns_of[2], 0, 0, 5)
-            relays(columns_of[3], 1, 0, 5)
-        if b == 1:
-            relays(columns_of[5], 1, 0, 4)
-            relays(columns_of[4], 0, 0, 5)
+        slot(b, "sent")
         kept = []
         for first, second, own, heard, out, seen, mine in (
             (a1, a2, sa, r1a, s1a, ys, y),
@@ -306,11 +337,7 @@
             for copy in first:
                 copy.wait_recv()
             if first is b1:
-                if b == 0:
-                    relays(columns_of[2], 0, 5)
-                    relays(columns_of[3], 1, 5)
-                if b == 1:
-                    relays(columns_of[4], 0, 5)
+                slot(b, "middle")
 
             def total_at(j):
                 total = own[b, NX - 1, j].astype(F32)
@@ -322,14 +349,7 @@
                 out[b, r] = total_at(seen[r]).astype(BF16)
                 second[r].start()
             kept.append(total_at(mine))
-        if b == 0:
-            launch(2, columns_of[4])
-            relays(columns_of[3], 0)
-            relays(columns_of[5], 0)
-            relays(columns_of[2], 1)
-        if b == 1:
-            relays(columns_of[5], 1, 4)
-            relays(columns_of[4], 1)
+        slot(b, "late")
         widen(b + 1)
         for rows, second, heard, total in ((rows_a, a2, r2a, kept[0]), (rows_b, b2, r2b, kept[1])):
             for r in range(NX - 1):
@@ -338,6 +358,8 @@
             state[rows, :] = (state[rows, :] + total).astype(BF16).astype(F32)
 
     for b in range(LIVE):
+        if b > 0:
+            slot(b - 1, "after")
         if b > 0:
             unfold(b)
             conv(b)
@@ -500,10 +522,8 @@
                 totals[way] = totals[way] + nt(left, right)
         return jnp.concatenate(totals, axis=0)
 
-    def home_copy(b, side, r, s):
-        return remote(
-            gsend.at[b, r, s], hrecv.at[side, r, s], gp_send.at[b], home_gp.at[side, r, s], (down, up)[side]
-        )
+    def home_copy(b, r, s):
+        return remote(gsend.at[b, r, s], hrecv.at[r, s], gp_send.at[b], home_gp.at[r, s], up)
 
     def gp_copy(b, r, s, device):
         return remote(gsend.at[b, r, s], crecv.at[b, r, s], gp_send.at[b], gp_recv.at[b, r, s], device)
@@ -533,28 +553,26 @@
                     @pl.when(jnp.logical_not(starter))
                     def _():
                         gpart[b % 2, r, s] = part
-                elif b > 0:
-                    far = is_z(b + 2)
-
-                    @pl.when(far)
+                elif slot < 2:
+                    @pl.when(z == b)
+                    def _():
+                        gpart[b % 2, r, s] = part
+
+                    @pl.when(z != b)
                     def _():
                         gsend[b, r, s] = part.astype(BF16)
-                        gp_copy(b, r, s, (down, up)[slot // 2]).start()
-
-                    if slot < 2:
-                        for side in range(2):
-                            @pl.when(is_z(b + starts[side]))
-                            def _():
-                                gsend[b, r, s] = part.astype(BF16)
-                                home_copy(b, side, r, s).start()
-
-                        @pl.when(z == b)
-                        def _():
-                            gpart[b % 2, r, s] = part
-                    else:
-                        @pl.when(jnp.logical_not(far))
-                        def _():
-                            gpart[b % 2, r, s] = part
+
+                    @pl.when(is_z(b + 1))
+                    def _():
+                        gp_copy(b, r, s, up).start()
+
+                    @pl.when(is_z(b + 2))
+                    def _():
+                        gp_copy(b, r, s, down).start()
+
+                    @pl.when(is_z(b + 3))
+                    def _():
+                        home_copy(b, slot, s).start()
                 else:
                     gpart[b % 2, r, s] = part
 
@@ -562,28 +580,15 @@
         def _():
             ghome[...] = gpart[b % 2]
 
-    def side_relay(b, lo, hi):
-        for j in range(lo, hi):
-            for side in range(2):
-                r, s = 2 * side + j // NY, j % NY
-
-                @pl.when(is_z(b + starts[side]))
-                def _():
-                    gp_copy(b, r, s, up).wait_recv()
-                    gsend[b, r, s] = (gpart[b % 2, r, s] + crecv[b, r, s].astype(F32)).astype(BF16)
-                    home_copy(b, side, r, s).start()
-
-    def point_relay(b, hop, lo, hi):
-        for j in range(lo, hi):
-            for way in range(2):
+    def point_relay(b, way, hop, lo, hi):
+        @pl.when(is_z(b + middles[way][hop]))
+        def _():
+            for j in range(lo, hi):
                 r, s = (2 if way == 0 else 0) + j // NY, j % NY
-
-                @pl.when(is_z(b + middles[way][hop]))
-                def _():
-                    copy = gp_copy(b, r, s, (up, down)[way])
-                    copy.wait_recv()
-                    gsend[b, r, s] = (gpart[b % 2, r, s] + crecv[b, r, s].astype(F32)).astype(BF16)
-                    copy.start()
+                copy = gp_copy(b, r, s, (up, down)[way])
+                copy.wait_recv()
+                gsend[b, r, s] = (gpart[b % 2, r, s] + crecv[b, r, s].astype(F32)).astype(BF16)
+                copy.start()
 
     silu_grad(LIVE, act_grad)
     back = (back + input_grad(LIVE)).astype(BF16).astype(F32)
@@ -604,23 +609,35 @@
     conv_weight_grad(LIVE)
     for b in range(LIVE - 1, -1, -1):
         if b + 2 < LIVE:
-            side_relay(b + 2, 0, 8)
+            point_relay(b + 2, 0, 1, 4, 8)
+        if b + 1 < LIVE:
+            point_relay(b + 1, 1, 1, 0, 2)
+            point_relay(b + 1, 0, 0, 0, 2)
         gather_third(links)
+        if b + 1 < LIVE:
+            point_relay(b + 1, 1, 1, 2, 6)
+            point_relay(b + 1, 0, 0, 2, 6)
         silu_grad(b, act_grad_of(b, links))
         if b > 0:
             back = (back + input_grad(b)).astype(BF16).astype(F32)
             links = gather_links(b - 1)
             gather_start(b - 1, links, back)
         point_grad(b)
+        if b + 1 < LIVE:
+            point_relay(b + 1, 1, 1, 6, 8)
+            point_relay(b + 1, 0, 0, 6, 8)
+            point_relay(b + 1, 0, 1, 0, 4)
         if b > 0:
             gather_second(links)
         conv_weight_grad(b)
-    side_relay(1, 0, 8)
-    for j in range(0, 8, 2):
-        point_relay(0, 0, j, j + 2)
-        if j:
-            point_relay(0, 1, j - 2, j)
-    point_relay(0, 1, 6, 8)
+    point_relay(1, 0, 1, 4, 8)
+    for j in range(8):
+        for way in range(2):
+            point_relay(0, way, 0, j, j + 1)
+            if j:
+                point_relay(0, way, 1, j - 1, j)
+    for way in range(2):
+        point_relay(0, way, 1, 7, 8)
 
     def out_copy(r, s):
         return pltpu.make_async_copy(
@@ -645,13 +662,11 @@
         def _():
             for j in range(2 * NY):
                 for r, s in ((2 + j // NY, j % NY), (j // NY, j % NY)):
-                    if b == 0:
-                        gp_copy(b, r, s, up).wait_recv()
-                        heard = crecv[b, r, s].astype(F32)
-                    else:
-                        for side in range(2):
-                            home_copy(b, side, r, s).wait_recv()
-                        heard = hrecv[0, r, s].astype(F32) + hrecv[1, r, s].astype(F32)
+                    gp_copy(b, r, s, up).wait_recv()
+                    heard = crecv[b, r, s].astype(F32)
+                    if b > 0 and r < 2:
+                        home_copy(b, r, s).wait_recv()
+                        heard = heard + hrecv[r, s].astype(F32)
                     ghome[r, s] = ghome[r, s] + heard
                     out_copy(r, s).start()
 
@@ -715,7 +730,7 @@
         V((LIVE, NY, NX, NC, part, width), BF16),
         V((LIVE, NX, NY, width, pair), BF16),
         V((LIVE, NX, NY, width, pair), BF16),
-        V((2, NX, NY, width, pair), BF16),
+        V((2, NY, width, pair), BF16),
         V((2, NX, NY, width, pair), F32),
         V((NX, NY, width, pair), F32),
         V((NZ, taps, group, width), BF16),
@@ -731,7 +746,7 @@
         dma((222,)),
         dma((LIVE,)),
         dma((LIVE, NX, NY)),
-        dma((2, NX, NY)),
+        dma((2, NY)),
         dma((4,)),
         dma((2,)),
     ]

time: 181 us -> 173 us (0.956)
  Pallas kernels: 175 us -> 167 us
    pallas_call x1, Pallas kernels: 175 us -> 167 us  [local(): pl.pallas_call(kernel, out_shape=(jax.ShapeDtypeStruct(point_weight.shape...]
where the time goes in v4:
time: 173 us
  Pallas kernels  167 us (97%)
  local copies, waits for them, and re-layouts  5.28 us (3%)
    pallas_call x1, Pallas kernels, local(): pl.pallas_call(kernel, out_shape=(jax.ShapeDtypeStruct(point_weight.shape...  167 us
    unnamed x5, local copies, waits for them, and re-layouts  5.28 us

profile of v4, /device:TPU:1, one launch (start us, length us, event | category | flops | bytes accessed | tf_op | source)
XLA Modules:
  0.0 172.7 jit_solution(13977149901640652925)
XLA Ops:
  0.6 1.4 copy.7.head_in
  2.0 166.8 %shard_map.68 = (f32[1,128,4096]{2,1,0:T(8,128)}, f32[1,9,64,128]{3,2,1,0:T(8,128)}) custom-call(bf16[4,256,128]{2,1,0:T(8,128)(2,1)} %inputs.1, s32[4,256]{1,0:T(4,128)} %labels_in.1, bf16[1,9,64,128]{3,2,1,0:T(8,128)(2,1)} %cw.1, bf16[1,128,4096]{2,1,0:T(8,128)(2,1)} %pw.1, bf16[128,3]{1,0:T(8,128)(2,1)} %copy.7.head_in), custom_call_target="tpu_custom_call" | custom-call | tf_op jit(solution)/shard_map/pallas_call | solution.py:753
  168.9 0.0 copy-start
  168.9 3.2 %copy.10 = f32[1,128,4096]{2,1,0:T(8,128)} copy(f32[1,128,4096]{2,1,0:T(8,128)} %get-tuple-element.4) | data formatting | bytes 4194304
  172.0 0.0 copy-done
  172.0 0.7 copy.11
Async XLA Ops:
  168.9 3.2 %copy-start = (f32[1,9,64,128]{3,2,1,0:T(8,128)S(1)}, f32[1,9,64,128]{3,2,1,0:T(8,128)}, u32[]{:S(2)}) copy-start(f32[1,9,64,128]{3,2,1,0:T(8,128)} %get-tuple-element.5) | copy-start | bytes 884740

commit v5 on v4

--- a/solution.py
+++ b/solution.py
@@ -256,22 +256,21 @@
 
     up1, down1, up2, down2 = columns_of[2:6]
     plan = {
-        (0, "early"): [(down1, 1, 0, 4), (up1, 0, 0, 1)],
-        (0, 1): [(down1, 1, 4, 5), (up1, 0, 1, 2)],
-        (0, 2): [(down1, 1, 5, 6), (up1, 0, 2, 3)],
-        (0, 3): [(up1, 0, 3, 4)],
-        (0, 4): [(down1, 1, 6, 7)],
-        (0, "sent"): [(down1, 1, 7, 8), (up1, 0, 4, 6), (up1, 1, 0, 2), (down2, 0, 0, 2)],
-        (0, "middle"): [(up1, 0, 6, 8), (up1, 1, 2, 5), (down2, 0, 2, 5)],
-        (0, "late"): [(up1, 1, 5, 8), (down2, 0, 5, 8)],
-        (1, "early"): [(down2, 1, 0, 5)],
-        (1, 1): [(down2, 1, 5, 6), (up2, 0, 0, 1)],
-        (1, 2): [(down2, 1, 6, 7), (up2, 0, 1, 2)],
-        (1, 3): [(down2, 1, 7, 8), (up2, 0, 2, 3)],
-        (1, "sent"): [(up2, 0, 3, 4), (up2, 1, 0, 1)],
-        (1, "middle"): [(up2, 0, 4, 7), (up2, 1, 1, 4)],
-        (1, "late"): [(up2, 0, 7, 8), (up2, 1, 4, 7)],
-        (1, "after"): [(up2, 1, 7, 8)],
+        (0, "early"): [(down1, 1, 0, 5), (up1, 0, 0, 2)],
+        (0, 1): [(down1, 1, 5, 6), (up1, 0, 2, 3)],
+        (0, 2): [(down1, 1, 6, 7), (up1, 0, 3, 4), (up1, 1, 0, 1)],
+        (0, 3): [(down1, 1, 7, 8), (up1, 0, 4, 5), (up1, 1, 1, 2)],
+        (0, 4): [(up1, 0, 5, 6), (up1, 1, 2, 3), (down2, 0, 0, 1)],
+        (0, "sent"): [(up1, 0, 6, 8), (up1, 1, 3, 6), (down2, 0, 1, 4)],
+        (0, "middle"): [(up1, 1, 6, 8), (down2, 0, 4, 7)],
+        (0, "late"): [(down2, 0, 7, 8)],
+        (1, "early"): [(down2, 1, 0, 6), (up2, 0, 0, 1)],
+        (1, 1): [(down2, 1, 6, 7), (up2, 0, 1, 2)],
+        (1, 2): [(down2, 1, 7, 8), (up2, 0, 2, 3), (up2, 1, 0, 1)],
+        (1, 3): [(up2, 0, 3, 4), (up2, 1, 1, 2)],
+        (1, "sent"): [(up2, 0, 4, 6), (up2, 1, 2, 4)],
+        (1, "middle"): [(up2, 0, 6, 8), (up2, 1, 4, 6)],
+        (1, "late"): [(up2, 1, 6, 8)],
     }
 
     def slot(b, name):
@@ -506,11 +505,12 @@
     def pair_cols(px, py):
         return pl.ds(pl.multiple_of((px * NY + py) * pair, pair), pair)
 
-    def act_grad_of(b, links):
+    def act_grad_of(b, links, waited=False):
         totals = [jnp.zeros((top_rows, width), F32) for _ in range(2)]
         for r in [NX - 1] + list(range(NX - 1)):
             for way, buffer in enumerate((ga, gb)):
-                links[("ca", "cb")[way]][r].wait_recv()
+                if not waited:
+                    links[("ca", "cb")[way]][r].wait_recv()
                 left = jnp.concatenate([buffer[b, r, s, k] for s in range(NY) for k in range(NC)], axis=1)
                 right = jnp.concatenate(
                     [
@@ -590,6 +590,11 @@
                 gsend[b, r, s] = (gpart[b % 2, r, s] + crecv[b, r, s].astype(F32)).astype(BF16)
                 copy.start()
 
+    def late_relays(b):
+        point_relay(b, 1, 1, 6, 8)
+        point_relay(b, 0, 0, 6, 8)
+        point_relay(b, 0, 1, 0, 4)
+
     silu_grad(LIVE, act_grad)
     back = (back + input_grad(LIVE)).astype(BF16).astype(F32)
     links = gather_links(LIVE - 1)
@@ -617,20 +622,24 @@
         if b + 1 < LIVE:
             point_relay(b + 1, 1, 1, 2, 6)
             point_relay(b + 1, 0, 0, 2, 6)
-        silu_grad(b, act_grad_of(b, links))
+        if b == 0:
+            for copy in links["ca"] + links["cb"]:
+                copy.wait_recv()
+            point_grad(0)
+            late_relays(1)
+            point_relay(1, 0, 1, 4, 6)
+        silu_grad(b, act_grad_of(b, links, b == 0))
         if b > 0:
             back = (back + input_grad(b)).astype(BF16).astype(F32)
             links = gather_links(b - 1)
             gather_start(b - 1, links, back)
-        point_grad(b)
-        if b + 1 < LIVE:
-            point_relay(b + 1, 1, 1, 6, 8)
-            point_relay(b + 1, 0, 0, 6, 8)
-            point_relay(b + 1, 0, 1, 0, 4)
+            point_grad(b)
+            if b + 1 < LIVE:
+                late_relays(b + 1)
         if b > 0:
             gather_second(links)
         conv_weight_grad(b)
-    point_relay(1, 0, 1, 4, 8)
+    point_relay(1, 0, 1, 6, 8)
     for j in range(8):
         for way in range(2):
             point_relay(0, way, 0, j, j + 1)

time: 173 us -> 169 us (0.977)
  Pallas kernels: 167 us -> 163 us
    pallas_call x1, Pallas kernels: 167 us -> 163 us  [local(): pl.pallas_call(kernel, out_shape=(jax.ShapeDtypeStruct(point_weight.shape...]
where the time goes in v5:
time: 169 us
  Pallas kernels  163 us (96%)
  local copies, waits for them, and re-layouts  5.28 us (3%)
    pallas_call x1, Pallas kernels, local(): pl.pallas_call(kernel, out_shape=(jax.ShapeDtypeStruct(point_weight.shape...  163 us
    unnamed x5, local copies, waits for them, and re-layouts  5.28 us

profile of v5, /device:TPU:1, one launch (start us, length us, event | category | flops | bytes accessed | tf_op | source)
XLA Modules:
  0.0 168.7 jit_solution(2142279150616755749)
XLA Ops:
  0.6 1.4 copy.7.head_in
  2.0 162.8 %shard_map.68 = (f32[1,128,4096]{2,1,0:T(8,128)}, f32[1,9,64,128]{3,2,1,0:T(8,128)}) custom-call(bf16[4,256,128]{2,1,0:T(8,128)(2,1)} %inputs.1, s32[4,256]{1,0:T(4,128)} %labels_in.1, bf16[1,9,64,128]{3,2,1,0:T(8,128)(2,1)} %cw.1, bf16[1,128,4096]{2,1,0:T(8,128)(2,1)} %pw.1, bf16[128,3]{1,0:T(8,128)(2,1)} %copy.7.head_in), custom_call_target="tpu_custom_call" | custom-call | tf_op jit(solution)/shard_map/pallas_call | solution.py:762
  164.8 0.0 copy-start
  164.8 3.2 %copy.10 = f32[1,128,4096]{2,1,0:T(8,128)} copy(f32[1,128,4096]{2,1,0:T(8,128)} %get-tuple-element.4) | data formatting | bytes 4194304
  168.0 0.0 copy-done
  168.0 0.7 copy.11
Async XLA Ops:
  164.8 3.2 %copy-start = (f32[1,9,64,128]{3,2,1,0:T(8,128)S(1)}, f32[1,9,64,128]{3,2,1,0:T(8,128)}, u32[]{:S(2)}) copy-start(f32[1,9,64,128]{3,2,1,0:T(8,128)} %get-tuple-element.5) | copy-start | bytes 884740

commit v6 on v5

--- a/solution.py
+++ b/solution.py
@@ -591,9 +591,9 @@
                 copy.start()
 
     def late_relays(b):
-        point_relay(b, 1, 1, 6, 8)
-        point_relay(b, 0, 0, 6, 8)
-        point_relay(b, 0, 1, 0, 4)
+        point_relay(b, 1, 1, 7, 8)
+        point_relay(b, 0, 0, 7, 8)
+        point_relay(b, 0, 1, 2, 4)
 
     silu_grad(LIVE, act_grad)
     back = (back + input_grad(LIVE)).astype(BF16).astype(F32)
@@ -616,12 +616,13 @@
         if b + 2 < LIVE:
             point_relay(b + 2, 0, 1, 4, 8)
         if b + 1 < LIVE:
-            point_relay(b + 1, 1, 1, 0, 2)
-            point_relay(b + 1, 0, 0, 0, 2)
+            point_relay(b + 1, 1, 1, 0, 3)
+            point_relay(b + 1, 0, 0, 0, 3)
         gather_third(links)
         if b + 1 < LIVE:
-            point_relay(b + 1, 1, 1, 2, 6)
-            point_relay(b + 1, 0, 0, 2, 6)
+            point_relay(b + 1, 1, 1, 3, 7)
+            point_relay(b + 1, 0, 0, 3, 7)
+            point_relay(b + 1, 0, 1, 0, 2)
         if b == 0:
             for copy in links["ca"] + links["cb"]:
                 copy.wait_recv()

time: 169 us -> 168 us (level)
  no operation moved by 1% of the time
where the time goes in v6:
time: 168 us
  Pallas kernels  162 us (96%)
  local copies, waits for them, and re-layouts  5.28 us (3%)
    pallas_call x1, Pallas kernels, local(): pl.pallas_call(kernel, out_shape=(jax.ShapeDtypeStruct(point_weight.shape...  162 us
    unnamed x5, local copies, waits for them, and re-layouts  5.28 us

profile of v6, /device:TPU:1, one launch (start us, length us, event | category | flops | bytes accessed | tf_op | source)
XLA Modules:
  0.0 168.1 jit_solution(2708335438051883209)
XLA Ops:
  0.6 1.4 copy.7.head_in
  2.0 162.2 %shard_map.68 = (f32[1,128,4096]{2,1,0:T(8,128)}, f32[1,9,64,128]{3,2,1,0:T(8,128)}) custom-call(bf16[4,256,128]{2,1,0:T(8,128)(2,1)} %inputs.1, s32[4,256]{1,0:T(4,128)} %labels_in.1, bf16[1,9,64,128]{3,2,1,0:T(8,128)(2,1)} %cw.1, bf16[1,128,4096]{2,1,0:T(8,128)(2,1)} %pw.1, bf16[128,3]{1,0:T(8,128)(2,1)} %copy.7.head_in), custom_call_target="tpu_custom_call" | custom-call | tf_op jit(solution)/shard_map/pallas_call | solution.py:763
  164.2 0.0 copy-start
  164.2 3.2 %copy.10 = f32[1,128,4096]{2,1,0:T(8,128)} copy(f32[1,128,4096]{2,1,0:T(8,128)} %get-tuple-element.4) | data formatting | bytes 4194304
  167.4 0.0 copy-done
  167.4 0.7 copy.11
Async XLA Ops:
  164.2 3.2 %copy-start = (f32[1,9,64,128]{3,2,1,0:T(8,128)S(1)}, f32[1,9,64,128]{3,2,1,0:T(8,128)}, u32[]{:S(2)}) copy-start(f32[1,9,64,128]{3,2,1,0:T(8,128)} %get-tuple-element.5) | copy-start | bytes 884740
